TPU v7x, 512 devices: a whole 4x4x16 slice. The times are simulated.
512 devices in a mesh: frame: 64 (over z_hi, y, x, core), head: 8 (over z_lo).
Axes of the slice: x: 4, y: 4, z: 16 (z_hi: 2, z_lo: 8; z = z_hi * 8 + z_lo), core: 2. Of those that a mesh axis runs over, the one named last changes fastest.
Arguments:
- latents: bfloat16 [64, 512, 3072], P('frame', 'head'), may hold values from -4 to 4
- queries: bfloat16 [64, 512, 3072], P('frame', 'head'), may hold values from -25 to 25
- keys: bfloat16 [64, 512, 3072], P('frame', 'head'), may hold values from -25 to 25
- values: bfloat16 [64, 512, 3072], P('frame', 'head'), may hold values from -6 to 6
- fresh: bfloat16 [512, 3072], P('head'), may hold values from -6 to 6
- timesteps: int32 [64], P('frame'), may hold values from 0 to 999
- window: int32 [64, 2], P('frame'), may hold values from 0 to 2, as said below
Outputs:
- denoised: bfloat16 [64, 512, 3072], P('frame', 'head')
- queue: bfloat16 [64, 512, 3072], P('frame', 'head')
Inputs may be any that keep to these rules, and one draw needn't show every extreme that they name: `window`: frame 64 - 1 has column 0 equal to 2; some frame has column 1 equal to 0.
All inputs are finite; a program needn't handle non-finite values.
Results may differ from a plain program's by a relative error of at most 0.012.
Values may be sent and summed in bfloat16 or wider, within the bound.
No kernel may reach another device: no remote copies, remote signals or barrier semaphores. Data moves between devices by JAX's collectives and lax.ppermute only.
A program may use at most 64 MiB of HBM per device.

v0:
```python
import jax
import jax.numpy as jnp
from jax import lax
from jax.sharding import PartitionSpec as P

HD = 64
REACH = 2
LEVELS = 1000


def from_behind(value, axis, steps):
    count = lax.axis_size(axis)
    leading, last = (max(0, -steps), min(count, count - steps))
    return lax.ppermute(value, axis, [(source, source + steps) for source in range(leading, last)])


def neighbours(stacked):
    earlier = []
    for distance in range(REACH, 0, -1):
        earlier.append(from_behind(stacked, "frame", distance))
    later = []
    for distance in range(1, REACH + 1):
        later.append(from_behind(stacked, "frame", -distance))
    return jnp.concatenate(earlier + [stacked] + later, axis=1)


def attend_heads(query, key_window, value_window, allowed):
    tokens_here = query.shape[0]
    head_count = query.shape[1] // HD
    span_rows = key_window.shape[0] * key_window.shape[1]
    query_heads = query.reshape(tokens_here, head_count, HD).transpose(1, 0, 2)
    key_heads = key_window.reshape(span_rows, head_count, HD).transpose(1, 0, 2)
    value_heads = value_window.reshape(span_rows, head_count, HD).transpose(1, 0, 2)
    usable = jnp.repeat(allowed, key_window.shape[1])

    def one_head(triple):
        query_head, key_head, value_head = triple
        scores = jnp.dot(query_head, key_head.T, preferred_element_type=jnp.float32) * HD ** (-0.5)
        scores = jnp.where(usable[None, :], scores, -jnp.inf)
        highest = jnp.max(scores, axis=1, keepdims=True)
        weights = jnp.exp(scores - highest)
        weights = (weights / jnp.sum(weights, axis=1, keepdims=True)).astype(jnp.bfloat16)
        return jnp.dot(weights, value_head, preferred_element_type=jnp.float32).astype(jnp.bfloat16)

    mixed = lax.map(one_head, (query_heads, key_heads, value_heads))
    return mixed.transpose(1, 0, 2).reshape(tokens_here, head_count * HD)


def per_device(latents, queries, keys, values, fresh, timesteps, window):
    frame_index = lax.axis_index("frame")
    frame_count = lax.axis_size("frame")
    extended = neighbours(jnp.stack((keys, values)))
    head_query, key_window, value_window = (
        lax.all_to_all(queries, "head", split_axis=2, concat_axis=1, tiled=True),
        lax.all_to_all(extended[0], "head", split_axis=2, concat_axis=1, tiled=True),
        lax.all_to_all(extended[1], "head", split_axis=2, concat_axis=1, tiled=True),
    )
    offsets = jnp.arange(-REACH, REACH + 1)
    target = frame_index + offsets
    allowed = (
        (target >= 0)
        & (target < frame_count)
        & (offsets >= -window[0, 0])
        & (offsets <= window[0, 1])
    )
    attended = attend_heads(head_query[0], key_window, value_window, allowed)
    returned = lax.all_to_all(attended[None], "head", split_axis=1, concat_axis=2, tiled=True)
    levels = timesteps.astype(jnp.float32) / LEVELS
    keep_share = (1.0 - 0.5 * levels)[:, None, None]
    push_share = (0.5 + levels)[:, None, None]
    denoised = (
        keep_share * latents.astype(jnp.float32) + push_share * returned.astype(jnp.float32)
    ).astype(jnp.bfloat16)
    advanced = from_behind(denoised, "frame", 1)
    return (denoised, jnp.where(frame_index == 0, fresh[None], advanced))


def solution(mesh):
    return jax.shard_map(
        per_device,
        mesh=mesh,
        in_specs=(
            P("frame", "head", None),
            P("frame", "head", None),
            P("frame", "head", None),
            P("frame", "head", None),
            P("head", None),
            P("frame"),
            P("frame", None),
        ),
        out_specs=(P("frame", "head", None), P("frame", "head", None)),
        check_vma=False,
    )
```

profile of v0, /device:TPU:288, one launch (start us, length us, event | category | flops | bytes accessed | tf_op | source)
XLA Modules:
  0.0 443.0 jit_solution(14711398111311078412)
XLA Ops:
  0.6 2.1 pad_maximum_fusion
  2.7 3.4 collective-permute-start
  6.1 1.9 collective-permute-start.1
  8.0 16.6 %collective-permute-start.2 = (bf16[2,1,64,3072]{3,2,1,0:T(8,128)(2,1)}, bf16[2,1,64,3072]{3,2,1,0:T(8,128)(2,1)}, u32[]{:S(2)}, u32[]{:S(2)}) collective-permute-start(bf16[2,1,64,3072]{3,2,1,0:T(8,128)(2,1)} %pad_maximum_fusion), channel_id=1, source_target_pairs={{8,0},{16,8},{24,16},{32,24},{40,32},{48,40},{56,48},{64,56},{72,6... | collective-permute-start | bytes 2359304 | tf_op jit(solution)/shard_map/ppermute | solution.py:14
  24.6 2.4 collective-permute-start.3
  27.1 3.6 copy.36
  31.2 17.0 %reduce = bf16[3072,64]{1,0:T(8,128)(2,1)S(1)} reduce(bf16[3072,1,64]{2,1,0:T(2,128)(2,1)S(1)} %bitcast.94, bf16[]{:T(256)} %broadcast.38), dimensions={1}, to_apply=%bitcast.64.reduce_sub_computation | reduce | bytes 786434
  48.2 1.3 reshape.47
  49.5 6.0 %all-to-all-start = ((bf16[8,2,12288]{2,1,0:T(2,128)(2,1)}), bf16[8,2,12288]{2,1,0:T(2,128)(2,1)S(1)}, u32[]{:S(2)}, u32[]{:S(2)}) async-start(bf16[8,2,12288]{2,1,0:T(2,128)(2,1)} %reshape.47), calls=%async_computation | async-start | bytes 786432 | tf_op jit(solution)/shard_map/all_to_all | solution.py:54
  55.5 64.9 %collective-permute-done = bf16[2,1,64,3072]{3,2,1,0:T(8,128)(2,1)} collective-permute-done((bf16[2,1,64,3072]{3,2,1,0:T(8,128)(2,1)}, bf16[2,1,64,3072]{3,2,1,0:T(8,128)(2,1)}, u32[]{:S(2)}, u32[]{:S(2)}) %collective-permute-start) | collective-permute-done | bytes 786464 | tf_op jit(solution)/shard_map/ppermute | solution.py:14
  120.4 1.2 constant_dynamic-update-slice_fusion.4
  121.6 6.6 %collective-permute-done.1 = bf16[2,1,64,3072]{3,2,1,0:T(8,128)(2,1)} collective-permute-done((bf16[2,1,64,3072]{3,2,1,0:T(8,128)(2,1)}, bf16[2,1,64,3072]{3,2,1,0:T(8,128)(2,1)}, u32[]{:S(2)}, u32[]{:S(2)}) %collective-permute-start.1) | collective-permute-done | bytes 786464 | tf_op jit(solution)/shard_map/ppermute | solution.py:14
  128.2 1.2 constant_dynamic-update-slice_fusion.3
  129.5 1.2 constant_dynamic-update-slice_fusion.1
  130.7 3.3 collective-permute-done.3
  134.0 1.2 constant_dynamic-update-slice_fusion
  135.2 1.7 slice_bitcast_fusion
  136.8 5.9 %copy.41 = bf16[5,64,3072]{1,0,2:T(8,128)(2,1)} copy(bf16[5,64,3072]{2,1,0:T(8,128)(2,1)S(1)} %get-tuple-element.88) | data formatting | bytes 3932160 | tf_op jit(solution)/shard_map/squeeze | solution.py:56
  142.8 8.3 %reshape.51 = bf16[8,2,61440]{2,1,0:T(2,128)(2,1)} reshape(bf16[3072,5,64]{2,1,0:T(8,128)(2,1)} %bitcast.89) | data formatting | bytes 3932160
  151.0 5.6 %all-to-all-start.2 = ((bf16[8,2,61440]{2,1,0:T(2,128)(2,1)}), bf16[8,2,61440]{2,1,0:T(2,128)(2,1)S(1)}, u32[]{:S(2)}, u32[]{:S(2)}) async-start(bf16[8,2,61440]{2,1,0:T(2,128)(2,1)} %reshape.51), calls=%async_computation.2 | async-start | bytes 3932160 | tf_op jit(solution)/shard_map/all_to_all | solution.py:56
  156.7 7.5 %copy.39 = bf16[5,64,3072]{1,0,2:T(8,128)(2,1)} copy(bf16[5,64,3072]{2,1,0:T(8,128)(2,1)} %get-tuple-element.89) | data formatting | bytes 3932160 | tf_op jit(solution)/shard_map/squeeze | solution.py:55
  164.2 8.2 %reshape.49 = bf16[8,2,61440]{2,1,0:T(2,128)(2,1)} reshape(bf16[3072,5,64]{2,1,0:T(8,128)(2,1)} %bitcast.90) | data formatting | bytes 3932160
  172.4 63.1 %all-to-all-done.2 = bf16[8,2,61440]{2,1,0:T(2,128)(2,1)S(1)} async-done(((bf16[8,2,61440]{2,1,0:T(2,128)(2,1)}), bf16[8,2,61440]{2,1,0:T(2,128)(2,1)S(1)}, u32[]{:S(2)}, u32[]{:S(2)}) %all-to-all-start.2) | async-done | bytes 1966112 | tf_op jit(solution)/shard_map/all_to_all | solution.py:56
  235.5 8.3 %all-to-all-start.1 = ((bf16[8,2,61440]{2,1,0:T(2,128)(2,1)}), bf16[8,2,61440]{2,1,0:T(2,128)(2,1)}, u32[]{:S(2)}, u32[]{:S(2)}) async-start(bf16[8,2,61440]{2,1,0:T(2,128)(2,1)} %reshape.49), calls=%async_computation.1 | async-start | bytes 3932160 | tf_op jit(solution)/shard_map/all_to_all | solution.py:55
  245.7 2.4 reshape.48
  248.1 2.7 copy.37
  250.8 1.0 copy.53
  253.0 5.9 %reshape.52 = bf16[3072,5,64]{2,1,0:T(8,128)(2,1)} reshape(bf16[8,2,61440]{2,1,0:T(2,128)(2,1)S(1)} %all-to-all-done.2) | data formatting | bytes 3932160
  258.9 9.3 %copy.57 = bf16[5,64,8,384]{1,2,0,3:T(8,128)(2,1)} copy(bf16[5,64,8,384]{1,0,3,2:T(8,128)(2,1)} %bitcast.87) | data formatting | bytes 3932160 | tf_op jit(solution)/shard_map/all_to_all | solution.py:56
  268.2 6.1 %reshape.46 = bf16[2560,6,64]{0,2,1:T(8,128)(2,1)} reshape(bf16[5,8,64,384]{2,1,0,3:T(8,128)(2,1)} %bitcast.91) | data formatting | bytes 3932160 | tf_op jit(solution)/shard_map/reshape | solution.py:33
  274.3 53.3 %all-to-all-done.1 = bf16[8,2,61440]{2,1,0:T(2,128)(2,1)} async-done(((bf16[8,2,61440]{2,1,0:T(2,128)(2,1)}), bf16[8,2,61440]{2,1,0:T(2,128)(2,1)}, u32[]{:S(2)}, u32[]{:S(2)}) %all-to-all-start.1) | async-done | bytes 1966112 | tf_op jit(solution)/shard_map/all_to_all | solution.py:55
  327.6 8.1 %reshape.50 = bf16[3072,5,64]{2,1,0:T(8,128)(2,1)} reshape(bf16[8,2,61440]{2,1,0:T(2,128)(2,1)} %all-to-all-done.1) | data formatting | bytes 3932160
  335.6 9.3 %copy.58 = bf16[5,64,8,384]{1,2,0,3:T(8,128)(2,1)} copy(bf16[5,64,8,384]{1,0,3,2:T(8,128)(2,1)} %bitcast.88) | data formatting | bytes 3932160 | tf_op jit(solution)/shard_map/all_to_all | solution.py:55
  344.9 5.2 %reshape.45 = bf16[2560,6,64]{0,2,1:T(8,128)(2,1)S(1)} reshape(bf16[5,8,64,384]{2,1,0,3:T(8,128)(2,1)} %bitcast.92) | data formatting | bytes 3932160 | tf_op jit(solution)/shard_map/reshape | solution.py:32
  350.1 24.4 %while.11 = (s32[]{:T(128)}, bf16[6,512,64]{1,2,0:T(8,128)(2,1)S(1)}, bf16[6,512,64]{1,2,0:T(8,128)(2,1)S(1)}, bf16[6,2560,64]{1,2,0:T(8,128)(2,1)S(1)}, bf16[6,...) while((s32[]{:T(128)}, bf16[6,512,64]{1,2,0:T(8,128)(2,1)S(1)}, ...), condition=%wide.region_3.4_spmd.clone, body=%wide.region_0.3_spmd.clone.sunk | while | flops 346061824 | bytes 16538194 | solution.py:45
  352.1 2.1 fusion.24
  354.3 1.0 fusion.22
  356.1 2.1 fusion.24
  360.2 2.1 fusion.24
  364.3 2.1 fusion.24
  368.3 2.1 fusion.24
  372.4 2.1 fusion.24
  374.5 1.1 copy.46
  375.6 3.0 reduce.1
  379.5 8.4 %all-to-all-start.3 = ((bf16[8,2,12288]{2,1,0:T(2,128)(2,1)}), bf16[8,2,12288]{2,1,0:T(2,128)(2,1)S(1)}, u32[]{:S(2)}, u32[]{:S(2)}) async-start(bf16[8,2,12288]{2,1,0:T(2,128)(2,1)} %reshape.53), calls=%async_computation.3 | async-start | bytes 786432 | tf_op jit(solution)/shard_map/all_to_all | solution.py:67
  388.5 19.5 %all-to-all-done.3 = bf16[8,2,12288]{2,1,0:T(2,128)(2,1)S(1)} async-done(((bf16[8,2,12288]{2,1,0:T(2,128)(2,1)}), bf16[8,2,12288]{2,1,0:T(2,128)(2,1)S(1)}, u32[]{:S(2)}, u32[]{:S(2)}) %all-to-all-start.3) | async-done | bytes 393248 | tf_op jit(solution)/shard_map/all_to_all | solution.py:67
  408.6 1.9 collective-permute-start.4
  410.5 31.7 %collective-permute-done.4 = bf16[1,64,3072]{2,1,0:T(8,128)(2,1)S(1)} collective-permute-done((bf16[1,64,3072]{2,1,0:T(8,128)(2,1)S(1)}, bf16[1,64,3072]{2,1,0:T(8,128)(2,1)S(1)}, u32[]{:S(2)}, u32[]{:S(2)}) %collective-permute-start.4) | collective-permute-done | bytes 393248 | tf_op jit(solution)/shard_map/ppermute | solution.py:14
  (55 shorter events, 15.8 us)
Async XLA Ops:
  2.7 117.7 %collective-permute-start = (bf16[2,1,64,3072]{3,2,1,0:T(8,128)(2,1)}, bf16[2,1,64,3072]{3,2,1,0:T(8,128)(2,1)}, u32[]{:S(2)}, u32[]{:S(2)}) collective-permute-start(bf16[2,1,64,3072]{3,2,1,0:T(8,128)(2,1)} %pad_maximum_fusion), channel_id=1, source_target_pairs={{0,16},{8,24},{16,32},{24,40},{32,48},{40,56},{48,64},{56,72},{64,... | collective-permute-start | bytes 2359304 | tf_op jit(solution)/shard_map/ppermute | solution.py:14
  6.1 122.1 %collective-permute-start.1 = (bf16[2,1,64,3072]{3,2,1,0:T(8,128)(2,1)}, bf16[2,1,64,3072]{3,2,1,0:T(8,128)(2,1)}, u32[]{:S(2)}, u32[]{:S(2)}) collective-permute-start(bf16[2,1,64,3072]{3,2,1,0:T(8,128)(2,1)} %pad_maximum_fusion), channel_id=1, source_target_pairs={{0,8},{8,16},{16,24},{24,32},{32,40},{40,48},{48,56},{56,64},{64,7... | collective-permute-start | bytes 2359304 | tf_op jit(solution)/shard_map/ppermute | solution.py:14
  8.0 121.5 %collective-permute-start.2 = (bf16[2,1,64,3072]{3,2,1,0:T(8,128)(2,1)}, bf16[2,1,64,3072]{3,2,1,0:T(8,128)(2,1)}, u32[]{:S(2)}, u32[]{:S(2)}) collective-permute-start(bf16[2,1,64,3072]{3,2,1,0:T(8,128)(2,1)} %pad_maximum_fusion), channel_id=1, source_target_pairs={{8,0},{16,8},{24,16},{32,24},{40,32},{48,40},{56,48},{64,56},{72,6... | collective-permute-start | bytes 2359304 | tf_op jit(solution)/shard_map/ppermute | solution.py:14
  24.6 109.3 %collective-permute-start.3 = (bf16[2,1,64,3072]{3,2,1,0:T(8,128)(2,1)}, bf16[2,1,64,3072]{3,2,1,0:T(8,128)(2,1)}, u32[]{:S(2)}, u32[]{:S(2)}) collective-permute-start(bf16[2,1,64,3072]{3,2,1,0:T(8,128)(2,1)} %pad_maximum_fusion), channel_id=1, source_target_pairs={{16,0},{24,8},{32,16},{40,24},{48,32},{56,40},{64,48},{72,56},{80,... | collective-permute-start | bytes 2359304 | tf_op jit(solution)/shard_map/ppermute | solution.py:14
  30.7 98.8 %copy-start = (bf16[1,64,3072]{2,1,0:T(8,128)(2,1)S(1)}, bf16[1,64,3072]{2,1,0:T(8,128)(2,1)}, u32[]{:S(2)}) copy-start(bf16[1,64,3072]{2,1,0:T(8,128)(2,1)} %param.12) | copy-start | bytes 1179652
  30.7 98.8 %copy-start.1 = (bf16[1,64,3072]{2,1,0:T(8,128)(2,1)S(1)}, bf16[1,64,3072]{2,1,0:T(8,128)(2,1)}, u32[]{:S(2)}) copy-start(bf16[1,64,3072]{2,1,0:T(8,128)(2,1)} %param.11) | copy-start | bytes 1179652
  49.5 101.6 %all-to-all-start = ((bf16[8,2,12288]{2,1,0:T(2,128)(2,1)}), bf16[8,2,12288]{2,1,0:T(2,128)(2,1)S(1)}, u32[]{:S(2)}, u32[]{:S(2)}) async-start(bf16[8,2,12288]{2,1,0:T(2,128)(2,1)} %reshape.47), calls=%async_computation | async-start | bytes 786432 | tf_op jit(solution)/shard_map/all_to_all | solution.py:54
  151.0 13.1 %copy-start.2 = (bf16[8,2,12288]{2,1,0:T(2,128)(2,1)}, bf16[8,2,12288]{2,1,0:T(2,128)(2,1)S(1)}, u32[]{:S(2)}) copy-start(bf16[8,2,12288]{2,1,0:T(2,128)(2,1)S(1)} %all-to-all-done) | copy-start | bytes 1179652
  151.0 84.4 %all-to-all-start.2 = ((bf16[8,2,61440]{2,1,0:T(2,128)(2,1)}), bf16[8,2,61440]{2,1,0:T(2,128)(2,1)S(1)}, u32[]{:S(2)}, u32[]{:S(2)}) async-start(bf16[8,2,61440]{2,1,0:T(2,128)(2,1)} %reshape.51), calls=%async_computation.2 | async-start | bytes 3932160 | tf_op jit(solution)/shard_map/all_to_all | solution.py:56
  172.4 71.4 %copy-start.7 = (s32[1,2]{1,0:T(1,128)S(1)}, s32[1,2]{1,0:T(1,128)}, u32[]{:S(2)}) copy-start(s32[1,2]{1,0:T(1,128)} %param.15) | copy-start | bytes 28
  235.5 92.1 %all-to-all-start.1 = ((bf16[8,2,61440]{2,1,0:T(2,128)(2,1)}), bf16[8,2,61440]{2,1,0:T(2,128)(2,1)}, u32[]{:S(2)}, u32[]{:S(2)}) async-start(bf16[8,2,61440]{2,1,0:T(2,128)(2,1)} %reshape.49), calls=%async_computation.1 | async-start | bytes 3932160 | tf_op jit(solution)/shard_map/all_to_all | solution.py:55
  344.9 5.2 %copy-start.5 = (bf16[6,512,64]{1,2,0:T(8,128)(2,1)S(1)}, bf16[6,512,64]{1,2,0:T(8,128)(2,1)}, u32[]{:S(2)}) copy-start(bf16[6,512,64]{1,2,0:T(8,128)(2,1)} %custom-call.1) | copy-start | bytes 1179652
  374.5 34.0 %copy-start.3 = (bf16[1,64,3072]{2,1,0:T(8,128)(2,1)S(1)}, bf16[1,64,3072]{2,1,0:T(8,128)(2,1)}, u32[]{:S(2)}) copy-start(bf16[1,64,3072]{2,1,0:T(8,128)(2,1)} %param.9) | copy-start | bytes 1179652
  378.6 63.6 %copy-start.4 = (bf16[64,3072]{1,0:T(8,128)(2,1)S(1)}, bf16[64,3072]{1,0:T(8,128)(2,1)}, u32[]{:S(2)}) copy-start(bf16[64,3072]{1,0:T(8,128)(2,1)} %param.13) | copy-start | bytes 1179652
  379.5 28.5 %all-to-all-start.3 = ((bf16[8,2,12288]{2,1,0:T(2,128)(2,1)}), bf16[8,2,12288]{2,1,0:T(2,128)(2,1)S(1)}, u32[]{:S(2)}, u32[]{:S(2)}) async-start(bf16[8,2,12288]{2,1,0:T(2,128)(2,1)} %reshape.53), calls=%async_computation.3 | async-start | bytes 786432 | tf_op jit(solution)/shard_map/all_to_all | solution.py:67
  408.6 34.4 %copy-start.6 = (bf16[1,64,3072]{2,1,0:T(8,128)(2,1)}, bf16[1,64,3072]{2,1,0:T(8,128)(2,1)S(1)}, u32[]{:S(2)}) copy-start(bf16[1,64,3072]{2,1,0:T(8,128)(2,1)S(1)} %add_convert_fusion) | copy-start | bytes 1179652
  408.6 33.6 %collective-permute-start.4 = (bf16[1,64,3072]{2,1,0:T(8,128)(2,1)S(1)}, bf16[1,64,3072]{2,1,0:T(8,128)(2,1)S(1)}, u32[]{:S(2)}, u32[]{:S(2)}) collective-permute-start(bf16[1,64,3072]{2,1,0:T(8,128)(2,1)S(1)} %add_convert_fusion), channel_id=1, source_target_pairs={{0,8},{8,16},{16,24},{24,32},{32,40},{40,48},{48,56},{56,64},{64,7... | collective-permute-start | bytes 1179656 | tf_op jit(solution)/shard_map/ppermute | solution.py:14
where the time goes:
time: 445 us; the launch traced here: 443 us
  waiting for transfers between devices  242 us (54%)
  local copies, waits for them, and re-layouts  96.4 us (22%)
  starting transfers between devices  54.6 us (12%)
  other arithmetic  28.7 us (6%)
  matrix products  18.6 us (4%)
    ppermute x5, waiting for transfers between devices, from_behind(): lax.ppermute(value, axis, [(source, source + steps) for source in range(l...  106 us
    all_to_all x1, waiting for transfers between devices, per_device(): lax.all_to_all(extended[1], 'head', split_axis=2, concat_axis=1, tiled=True)  63.1 us
    all_to_all x1, waiting for transfers between devices, per_device(): lax.all_to_all(extended[0], 'head', split_axis=2, concat_axis=1, tiled=True)  53.3 us
    unnamed x30, local copies, waits for them, and re-layouts  44.1 us
    ppermute x5, starting transfers between devices, from_behind(): lax.ppermute(value, axis, [(source, source + steps) for source in range(l...  26.3 us
    unnamed x3, other arithmetic  20 us
    all_to_all x1, waiting for transfers between devices, per_device(): lax.all_to_all(attended[None], 'head', split_axis=1, concat_axis=2, tiled...  19.5 us
    dot_general x6, matrix products, one_head(): jnp.dot(weights, value_head, preferred_element_type=jnp.float32)  12.6 us
  transfers between devices with their start and end apart: 9, of which 7 were waited for; matrix products, arithmetic and copies ran while one was open for 20% of the time, Pallas kernels for 0%

commit v1 on v0

v1 whole, which is shorter than its diff:
```python
import functools

import jax
import jax.numpy as jnp
from jax import lax
from jax.experimental import pallas as pl
from jax.experimental.pallas import tpu as pltpu
from jax.sharding import PartitionSpec as P

HD = 64
REACH = 2
LEVELS = 1000
SLOTS = 2 * REACH + 1
PAIR = 2 * HD
LOG2E = 1.4426950408889634
AXES = ("frame", "head")


def head_split_kernel(groups, width, flip_ref, *refs):
    inputs, out_ref, sem = refs[:-2], refs[-2], refs[-1]
    flip = flip_ref[0]
    copies = []
    for block in range(groups):
        group = jnp.where(flip == 1, groups - 1 - block, block)
        columns = pl.ds(pl.multiple_of(group * width, 128), width)
        for index, source in enumerate(inputs):
            copies.append(
                pltpu.make_async_copy(source.at[:, columns], out_ref.at[block, index], sem.at[block, index])
            )
    for copy in copies:
        copy.start()
    for copy in copies:
        copy.wait()


def head_split(flip, groups, *arrays):
    rows, columns = arrays[0].shape
    width = columns // groups
    count = len(arrays)
    size = count * rows * columns * 2
    return pl.pallas_call(
        functools.partial(head_split_kernel, groups, width),
        out_shape=jax.ShapeDtypeStruct((groups, count, rows, width), jnp.bfloat16),
        in_specs=[pl.BlockSpec(memory_space=pltpu.SMEM)] + [pl.BlockSpec(memory_space=pl.ANY)] * count,
        out_specs=pl.BlockSpec(memory_space=pl.ANY),
        scratch_shapes=[pltpu.SemaphoreType.DMA((groups, count))],
        cost_estimate=pl.CostEstimate(flops=0, bytes_accessed=2 * size, transcendentals=0),
    )(flip, *arrays)


def attention_kernel(
    blocks, pairs, rows, picks_ref, q_ref, own, back2, back1, next1, next2, cross, cross_near,
    out_ref, k_buf, v_buf, score, high, total, sem,
):
    per_block = own.shape[2]
    span = blocks * per_block

    def copies(source, slot, pair):
        found = []
        for which, buf in enumerate((k_buf, v_buf)):
            for block in range(blocks):
                found.append(
                    pltpu.make_async_copy(
                        source.at[block, which, :, pl.ds(pair * PAIR, PAIR)],
                        buf.at[pair, slot, pl.ds(block * per_block, per_block), pl.ds(0, PAIR)],
                        sem.at[pair, slot],
                    )
                )
        return found

    sources = (back2, back1, own, next1, next2)
    crossing = (cross, cross_near, None, cross_near, cross)
    for pair in range(pairs):
        for slot in range(SLOTS):
            @pl.when(picks_ref[slot] == 1)
            def _(pair=pair, slot=slot):
                for copy in copies(sources[slot], slot, pair):
                    copy.start()

            if crossing[slot] is not None:
                @pl.when(picks_ref[slot] == 2)
                def _(pair=pair, slot=slot):
                    for copy in copies(crossing[slot], slot, pair):
                        copy.start()

    v_buf[:, :, :, PAIR:] = jnp.ones((pairs, SLOTS, span, PAIR), jnp.bfloat16)
    lane = lax.broadcasted_iota(jnp.int32, (rows, PAIR), 1)
    for pair in range(pairs):
        for slot in range(SLOTS):
            @pl.when(picks_ref[slot] > 0)
            def _(pair=pair, slot=slot):
                for copy in copies(sources[slot], slot, pair):
                    copy.wait()

        for chunk in range(span // rows):
            per_chunk = rows // per_block
            query = q_ref[chunk * per_chunk : (chunk + 1) * per_chunk, 0, :, pair * PAIR : (pair + 1) * PAIR]
            query = query.reshape(rows, PAIR)
            zero = jnp.zeros_like(query)
            both = jnp.concatenate(
                [jnp.where(lane < HD, query, zero), jnp.where(lane < HD, zero, query)], axis=0
            )
            high[...] = jnp.full(high.shape, -jnp.inf, jnp.float32)
            total[...] = jnp.zeros(total.shape, jnp.float32)
            for slot in range(SLOTS):
                @pl.when(picks_ref[slot] > 0)
                def _(pair=pair, slot=slot):
                    found = lax.dot_general(
                        both, k_buf[pair, slot], (((1,), (1,)), ((), ())), preferred_element_type=jnp.float32
                    )
                    score[slot] = found
                    high[...] = jnp.maximum(high[...], jnp.max(found, axis=1, keepdims=True))
            for slot in range(SLOTS):
                @pl.when(picks_ref[slot] > 0)
                def _(pair=pair, slot=slot):
                    weights = jnp.exp2((score[slot] - high[...]) * (HD ** -0.5 * LOG2E)).astype(jnp.bfloat16)
                    total[...] += jnp.dot(weights, v_buf[pair, slot], preferred_element_type=jnp.float32)
            mixed = total[:, :PAIR] / total[:, PAIR:]
            mixed = jnp.where(lane < HD, mixed[:rows], mixed[rows:]).astype(jnp.bfloat16)
            out_ref[chunk * per_chunk : (chunk + 1) * per_chunk, :, pair * PAIR : (pair + 1) * PAIR] = mixed.reshape(
                per_chunk, per_block, PAIR
            )


def attend(picks, query, own, back2, back1, next1, next2, cross, cross_near):
    blocks, _, per_block, width = query.shape
    pairs = width // PAIR
    span = blocks * per_block
    rows = 256
    return pl.pallas_call(
        functools.partial(attention_kernel, blocks, pairs, rows),
        out_shape=jax.ShapeDtypeStruct((blocks, per_block, width), jnp.bfloat16),
        in_specs=[pl.BlockSpec(memory_space=pltpu.SMEM), pl.BlockSpec(memory_space=pltpu.VMEM)]
        + [pl.BlockSpec(memory_space=pl.ANY)] * 7,
        out_specs=pl.BlockSpec(memory_space=pltpu.VMEM),
        scratch_shapes=[
            pltpu.VMEM((pairs, SLOTS, span, PAIR), jnp.bfloat16),
            pltpu.VMEM((pairs, SLOTS, span, 2 * PAIR), jnp.bfloat16),
            pltpu.VMEM((SLOTS, 2 * rows, span), jnp.float32),
            pltpu.VMEM((2 * rows, 1), jnp.float32),
            pltpu.VMEM((2 * rows, 2 * PAIR), jnp.float32),
            pltpu.SemaphoreType.DMA((pairs, SLOTS)),
        ],
        compiler_params=pltpu.CompilerParams(vmem_limit_bytes=40 * 1024 * 1024),
        cost_estimate=pl.CostEstimate(
            flops=4 * span * span * SLOTS * width,
            bytes_accessed=(2 * SLOTS + 2) * span * width * 2,
            transcendentals=span * span * SLOTS * width // HD,
        ),
    )(picks, query, own, back2, back1, next1, next2, cross, cross_near)


def blend_kernel(groups, width, flip_ref, share_ref, latents_ref, returned_ref, out_ref):
    flip = flip_ref[0]
    for group in range(groups):
        block = jnp.where(flip == 1, groups - 1 - group, group)
        columns = slice(group * width, (group + 1) * width)
        out_ref[:, columns] = (
            share_ref[0] * latents_ref[:, columns].astype(jnp.float32)
            + share_ref[1] * returned_ref[block].astype(jnp.float32)
        ).astype(jnp.bfloat16)


def blend(flip, shares, latents, returned):
    groups, rows, width = returned.shape
    return pl.pallas_call(
        functools.partial(blend_kernel, groups, width),
        out_shape=jax.ShapeDtypeStruct(latents.shape, jnp.bfloat16),
        in_specs=[pl.BlockSpec(memory_space=pltpu.SMEM)] * 2 + [pl.BlockSpec(memory_space=pltpu.VMEM)] * 2,
        out_specs=pl.BlockSpec(memory_space=pltpu.VMEM),
        cost_estimate=pl.CostEstimate(flops=3 * latents.size, bytes_accessed=6 * latents.size, transcendentals=0),
    )(flip, shares, latents, returned)


def per_device(frames, heads, latents, queries, keys, values, fresh, timesteps, window):
    frame = lax.axis_index("frame")
    half = frames // 2
    flip = (frame >= half).astype(jnp.int32)[None]

    def mirrored(moves):
        return [
            (a * heads + z, b * heads + (heads - 1 - z)) for a, b in moves for z in range(heads)
        ]

    def straight(moves):
        return [(a * heads + z, b * heads + z) for a, b in moves for z in range(heads)]

    def within(distance):
        return straight(
            [(f, f + distance) for f in range(frames) if 0 <= f + distance < frames and (f < half) == (f + distance < half)]
        )

    send = lambda value, moves: lax.ppermute(value, AXES, moves)
    exchange = lambda value: lax.all_to_all(value, "head", split_axis=0, concat_axis=0, tiled=True)

    own = exchange(head_split(flip, heads, keys, values))
    query = head_split(flip, heads, queries)
    own, query = lax.optimization_barrier((own, query))

    mid = heads // 2
    cross_a = send(own[:mid], mirrored([(half - 2, half), (half - 1, half + 1), (half + 1, half - 1), (half, half - 2)]))
    relay = send(
        own[mid:], straight([(half - 2, half - 4), (half - 1, half - 3), (half + 1, half + 3), (half, half + 2)])
    )
    cross_b = send(relay, mirrored([(half - 4, half), (half - 3, half + 1), (half + 3, half - 1), (half + 2, half - 2)]))
    back2 = send(own, within(2))
    next2 = send(own, within(-2))
    back1 = send(own, within(1))
    next1 = send(own, within(-1))
    cross = jnp.concatenate([cross_a, cross_b])
    cross_near = send(cross, straight([(half + 1, half), (half - 2, half - 1)]))

    query = exchange(query)

    offsets = jnp.arange(-REACH, REACH + 1)
    target = frame + offsets
    allowed = (
        (target >= 0) & (target < frames) & (offsets >= -window[0, 0]) & (offsets <= window[0, 1])
    )
    picks = jnp.where(allowed, jnp.where((target < half) == (frame < half), 1, 2), 0).astype(jnp.int32)
    attended = attend(picks, query, own, back2, back1, next1, next2, cross, cross_near)
    returned = exchange(attended)
    levels = timesteps.astype(jnp.float32) / LEVELS
    shares = jnp.concatenate([1.0 - 0.5 * levels, 0.5 + levels])
    denoised = blend(flip, shares, latents[0], returned)[None]
    advanced = send(denoised, straight([(f, f + 1) for f in range(frames - 1)]))
    return (denoised, jnp.where(frame == 0, fresh[None], advanced))


def solution(mesh):
    def body(latents, queries, keys, values, fresh, timesteps, window):
        return per_device(
            mesh.shape["frame"], mesh.shape["head"], latents, queries[0], keys[0], values[0], fresh, timesteps, window
        )

    return jax.shard_map(
        body,
        mesh=mesh,
        in_specs=(
            P("frame", "head", None),
            P("frame", "head", None),
            P("frame", "head", None),
            P("frame", "head", None),
            P("head", None),
            P("frame"),
            P("frame", None),
        ),
        out_specs=(P("frame", "head", None), P("frame", "head", None)),
        check_vma=False,
    )
```

time: 445 us -> 217 us (0.49)
  waiting for transfers between devices: 242 us -> 99.6 us
  local copies, waits for them, and re-layouts: 96.4 us -> 3.33 us
  Pallas kernels: 0 us -> 61.3 us
  other arithmetic: 28.7 us -> 2.01 us
  matrix products: 18.6 us -> 0 us
  starting transfers between devices: 54.6 us -> 47.8 us
    all_to_all x4 -> x3, waiting for transfers between devices: 136 us -> 38.2 us  [per_device(): lax.all_to_all(value, 'head', split_axis=0, concat_axis=0, tiled=True)]
    pallas_call x0 -> x4, Pallas kernels: none -> 61.3 us  [the longest x2 38.2 us: head_split(): pl.pallas_call(functools.partial(head_split_kernel, groups, width), out_s...]
    ppermute x5 -> x9, waiting for transfers between devices: 106 us -> 61.4 us  [per_device(): send = lambda value, moves: lax.ppermute(value, AXES, moves)]
    unnamed x30 -> x9, local copies, waits for them, and re-layouts: 44.1 us -> 2.54 us
    all_to_all x5 -> x0, local copies, waits for them, and re-layouts: 22 us -> none  [the longest x1 9.29 us: per_device(): lax.all_to_all(extended[1], 'head', split_axis=2, concat_axis=1, tiled=True)]
    unnamed x3 -> x0, other arithmetic: 20 us -> none
    dot_general x12 -> x0, matrix products: 18.6 us -> none  [the longest x6 12.6 us: one_head(): jnp.dot(weights, value_head, preferred_element_type=jnp.float32)]
    squeeze x3 -> x0, local copies, waits for them, and re-layouts: 15.2 us -> none  [the longest x2 7.63 us: per_device(): extended[1]]
  transfers between devices with their start and end apart: 9 -> 12, of which waited for: 7 -> 6; matrix products, arithmetic and copies ran while one was open for 20% -> 1% of each run, Pallas kernels for 0% -> 6%
where the time goes in v1:
time: 217 us; the launch traced here: 216 us
  waiting for transfers between devices  99.6 us (46%)
  Pallas kernels  61.3 us (28%)
  starting transfers between devices  47.8 us (22%)
  local copies, waits for them, and re-layouts  3.33 us (2%)
    ppermute x9, waiting for transfers between devices, per_device(): send = lambda value, moves: lax.ppermute(value, AXES, moves)  61.4 us
    all_to_all x3, waiting for transfers between devices, per_device(): lax.all_to_all(value, 'head', split_axis=0, concat_axis=0, tiled=True)  38.2 us
    pallas_call x2, Pallas kernels, head_split(): pl.pallas_call(functools.partial(head_split_kernel, groups, width), out_s...  38.2 us
    all_to_all x3, starting transfers between devices, per_device(): lax.all_to_all(value, 'head', split_axis=0, concat_axis=0, tiled=True)  25.2 us
    ppermute x9, starting transfers between devices, per_device(): send = lambda value, moves: lax.ppermute(value, AXES, moves)  22.6 us
    pallas_call x1, Pallas kernels, attend(): pl.pallas_call(functools.partial(attention_kernel, blocks, pairs, rows),...  21.1 us
  transfers between devices with their start and end apart: 12, of which 6 were waited for; matrix products, arithmetic and copies ran while one was open for 1% of the time, Pallas kernels for 6%

profile of v1, /device:TPU:288, one launch (start us, length us, event | category | flops | bytes accessed | tf_op | source)
XLA Modules:
  0.0 216.2 jit_solution(1366594963138616807)
XLA Ops:
  0.6 25.1 %shard_map.86 = bf16[8,2,64,384]{3,2,1,0:T(8,128)(2,1)} custom-call(s32[1]{0:T(128)} %bitcast.flip_ref, bf16[64,3072]{1,0:T(8,128)(2,1)} %bitcast.10, bf16[64,3072]{1,0:T(8,128)(2,1)} %bitcast.11), custom_call_target="tpu_custom_call" | custom-call | bytes 1572864 | tf_op jit(solution)/shard_map/pallas_call | solution.py:41
  25.7 6.0 %all-to-all-start = ((bf16[8,2,64,384]{3,2,1,0:T(8,128)(2,1)}), bf16[8,2,64,384]{3,2,1,0:T(8,128)(2,1)S(1)}, u32[]{:S(2)}, u32[]{:S(2)}) async-start(bf16[8,2,64,384]{3,2,1,0:T(8,128)(2,1)} %shard_map.86), calls=%async_computation | async-start | bytes 1572864 | tf_op jit(solution)/shard_map/all_to_all | solution.py:194
  31.8 13.1 %shard_map.87 = bf16[8,1,64,384]{3,2,1,0:T(8,128)(2,1)} custom-call(s32[1]{0:T(128)} %bitcast.flip_ref, bf16[64,3072]{1,0:T(8,128)(2,1)} %bitcast.12), custom_call_target="tpu_custom_call" | custom-call | bytes 786432 | tf_op jit(solution)/shard_map/pallas_call | solution.py:41
  44.8 24.4 %all-to-all-done.own = bf16[8,2,64,384]{3,2,1,0:T(8,128)(2,1)S(1)} async-done(((bf16[8,2,64,384]{3,2,1,0:T(8,128)(2,1)}), bf16[8,2,64,384]{3,2,1,0:T(8,128)(2,1)S(1)}, u32[]{:S(2)}, u32[]{:S(2)}) %all-to-all-start) | async-done | bytes 786464 | tf_op jit(solution)/shard_map/all_to_all | solution.py:194
  69.2 0.1 fusion
  69.3 4.2 %collective-permute-start.5 = (bf16[4,2,64,384]{3,2,1,0:T(8,128)(2,1)S(1)}, bf16[4,2,64,384]{3,2,1,0:T(8,128)(2,1)}, u32[]{:S(2)}, u32[]{:S(2)}) collective-permute-start(bf16[4,2,64,384]{3,2,1,0:T(8,128)(2,1)S(1)} %get-tuple-element.6), channel_id=1, source_target_pairs={{240,224},{241,225},{242,226},{243,227},{244,228},{245,229},{246,2... | collective-permute-start | bytes 1179656 | tf_op jit(solution)/shard_map/ppermute | solution.py:193
  73.5 5.2 %collective-permute-start.4 = (bf16[4,2,64,384]{3,2,1,0:T(8,128)(2,1)S(1)}, bf16[4,2,64,384]{3,2,1,0:T(8,128)(2,1)S(1)}, u32[]{:S(2)}, u32[]{:S(2)}) collective-permute-start(bf16[4,2,64,384]{3,2,1,0:T(8,128)(2,1)S(1)} %get-tuple-element.7), channel_id=1, source_target_pairs={{240,263},{241,262},{242,261},{243,260},{244,259},{245,258},{246,2... | collective-permute-start | bytes 1179656 | tf_op jit(solution)/shard_map/ppermute | solution.py:193
  78.7 9.5 %all-to-all-start.1 = ((bf16[8,1,64,384]{3,2,1,0:T(8,128)(2,1)}), bf16[8,1,64,384]{3,2,1,0:T(8,128)(2,1)S(1)}, u32[]{:S(2)}, u32[]{:S(2)}) async-start(bf16[8,1,64,384]{3,2,1,0:T(8,128)(2,1)} %shard_map.87), calls=%async_computation.1 | async-start | bytes 786432 | tf_op jit(solution)/shard_map/all_to_all | solution.py:194
  88.2 0.0 collective-permute-done.5
  88.2 1.3 collective-permute-start.6
  89.4 1.3 collective-permute-start.3
  90.7 1.3 collective-permute-start.2
  92.0 4.0 %collective-permute-start.1 = (bf16[8,2,64,384]{3,2,1,0:T(8,128)(2,1)S(1)}, bf16[8,2,64,384]{3,2,1,0:T(8,128)(2,1)}, u32[]{:S(2)}, u32[]{:S(2)}) collective-permute-start(bf16[8,2,64,384]{3,2,1,0:T(8,128)(2,1)S(1)} %all-to-all-done.own), channel_id=1, source_target_pairs={{0,8},{1,9},{2,10},{3,11},{4,12},{5,13},{6,14},{7,15},{8,16},{9,17... | collective-permute-start | bytes 2359304 | tf_op jit(solution)/shard_map/ppermute | solution.py:193
  96.0 17.7 %collective-permute-done.4 = bf16[4,2,64,384]{3,2,1,0:T(8,128)(2,1)S(1)} collective-permute-done((bf16[4,2,64,384]{3,2,1,0:T(8,128)(2,1)S(1)}, bf16[4,2,64,384]{3,2,1,0:T(8,128)(2,1)S(1)}, u32[]{:S(2)}, u32[]{:S(2)}) %collective-permute-start.4) | collective-permute-done | bytes 393248 | tf_op jit(solution)/shard_map/ppermute | solution.py:193
  113.7 0.0 copy-start.1
  113.7 0.7 copy-done.1
  114.4 2.2 %collective-permute-start = (bf16[8,2,64,384]{3,2,1,0:T(8,128)(2,1)S(1)}, bf16[8,2,64,384]{3,2,1,0:T(8,128)(2,1)}, u32[]{:S(2)}, u32[]{:S(2)}) collective-permute-start(bf16[8,2,64,384]{3,2,1,0:T(8,128)(2,1)S(1)} %all-to-all-done.own), channel_id=1, source_target_pairs={{0,16},{1,17},{2,18},{3,19},{4,20},{5,21},{6,22},{7,23},{8,24},{9,... | collective-permute-start | bytes 2359304 | tf_op jit(solution)/shard_map/ppermute | solution.py:193
  116.6 1.0 constant_dynamic-update-slice_fusion.1
  117.6 6.3 %collective-permute-done.6 = bf16[4,2,64,384]{3,2,1,0:T(8,128)(2,1)S(1)} collective-permute-done((bf16[4,2,64,384]{3,2,1,0:T(8,128)(2,1)}, bf16[4,2,64,384]{3,2,1,0:T(8,128)(2,1)S(1)}, u32[]{:S(2)}, u32[]{:S(2)}) %collective-permute-start.6) | collective-permute-done | bytes 393248 | tf_op jit(solution)/shard_map/ppermute | solution.py:193
  123.9 0.1 constant_dynamic-update-slice_fusion.cross
  124.0 0.0 copy-start.3
  124.0 1.3 collective-permute-start.7
  125.3 0.0 copy-done.3
  125.3 0.6 fusion.1
  126.6 0.6 and_select_fusion.picks_ref
  127.3 0.0 collective-permute-done.3.next2
  127.3 0.0 collective-permute-done.2.next1
  127.3 0.0 collective-permute-done.1.back1
  127.3 5.6 %collective-permute-done.back2 = bf16[8,2,64,384]{3,2,1,0:T(8,128)(2,1)} collective-permute-done((bf16[8,2,64,384]{3,2,1,0:T(8,128)(2,1)S(1)}, bf16[8,2,64,384]{3,2,1,0:T(8,128)(2,1)}, u32[]{:S(2)}, u32[]{:S(2)}) %collective-permute-start) | collective-permute-done | bytes 786464 | tf_op jit(solution)/shard_map/ppermute | solution.py:193
  132.9 0.0 all-to-all-done.1.q_ref
  132.9 0.0 collective-permute-done.7.cross_near
  132.9 21.1 %shard_map.88 = bf16[8,64,384]{2,1,0:T(8,128)(2,1)} custom-call(s32[5]{0:T(128)S(1)} %and_select_fusion.picks_ref, bf16[8,1,64,384]{3,2,1,0:T(8,128)(2,1)S(1)} %all-to-all-done.1.q_ref, bf16[8,2,64,384]{3,2,1,0:T(8,128)(2,1)S(1)} %all-to-all-done.own, bf16[8,2,64,384]{3,2,1,0:T(8,128)(2,1)} %collective-permute-done.back2, ...), custom_call_target="tpu_custom_call" | custom-call | flops 2013265920 | bytes 4718592 | tf_op jit(solution)/shard_map/pallas_call | solution.py:130
  154.0 9.7 %all-to-all-start.2 = ((bf16[8,64,384]{2,1,0:T(8,128)(2,1)}), bf16[8,64,384]{2,1,0:T(8,128)(2,1)S(1)}, u32[]{:S(2)}, u32[]{:S(2)}) async-start(bf16[8,64,384]{2,1,0:T(8,128)(2,1)} %shard_map.88), calls=%async_computation.2 | async-start | bytes 786432 | tf_op jit(solution)/shard_map/all_to_all | solution.py:194
  164.4 0.6 pad_maximum_fusion.share_ref
  165.0 13.8 %all-to-all-done.2.returned_ref = bf16[8,64,384]{2,1,0:T(8,128)(2,1)S(1)} async-done(((bf16[8,64,384]{2,1,0:T(8,128)(2,1)}), bf16[8,64,384]{2,1,0:T(8,128)(2,1)S(1)}, u32[]{:S(2)}, u32[]{:S(2)}) %all-to-all-start.2) | async-done | bytes 393248 | tf_op jit(solution)/shard_map/all_to_all | solution.py:194
  178.8 0.0 copy-start
  178.8 0.7 copy-done
  179.5 0.0 copy-start.2
  179.5 2.1 shard_map.89
  181.6 1.9 collective-permute-start.8
  183.5 31.9 %collective-permute-done.8 = bf16[1,64,3072]{2,1,0:T(8,128)(2,1)S(1)} collective-permute-done((bf16[1,64,3072]{2,1,0:T(8,128)(2,1)}, bf16[1,64,3072]{2,1,0:T(8,128)(2,1)S(1)}, u32[]{:S(2)}, u32[]{:S(2)}) %collective-permute-start.8) | collective-permute-done | bytes 393248 | tf_op jit(solution)/shard_map/ppermute | solution.py:193
  215.4 0.0 copy-done.2
  215.4 0.8 bitcast_select_fusion
Async XLA Ops:
  25.7 43.5 %all-to-all-start = ((bf16[8,2,64,384]{3,2,1,0:T(8,128)(2,1)}), bf16[8,2,64,384]{3,2,1,0:T(8,128)(2,1)S(1)}, u32[]{:S(2)}, u32[]{:S(2)}) async-start(bf16[8,2,64,384]{3,2,1,0:T(8,128)(2,1)} %shard_map.86), calls=%async_computation | async-start | bytes 1572864 | tf_op jit(solution)/shard_map/all_to_all | solution.py:194
  69.3 18.9 %collective-permute-start.5 = (bf16[4,2,64,384]{3,2,1,0:T(8,128)(2,1)S(1)}, bf16[4,2,64,384]{3,2,1,0:T(8,128)(2,1)}, u32[]{:S(2)}, u32[]{:S(2)}) collective-permute-start(bf16[4,2,64,384]{3,2,1,0:T(8,128)(2,1)S(1)} %get-tuple-element.6), channel_id=1, source_target_pairs={{240,224},{241,225},{242,226},{243,227},{244,228},{245,229},{246,2... | collective-permute-start | bytes 1179656 | tf_op jit(solution)/shard_map/ppermute | solution.py:193
  73.5 40.2 %collective-permute-start.4 = (bf16[4,2,64,384]{3,2,1,0:T(8,128)(2,1)S(1)}, bf16[4,2,64,384]{3,2,1,0:T(8,128)(2,1)S(1)}, u32[]{:S(2)}, u32[]{:S(2)}) collective-permute-start(bf16[4,2,64,384]{3,2,1,0:T(8,128)(2,1)S(1)} %get-tuple-element.7), channel_id=1, source_target_pairs={{240,263},{241,262},{242,261},{243,260},{244,259},{245,258},{246,2... | collective-permute-start | bytes 1179656 | tf_op jit(solution)/shard_map/ppermute | solution.py:193
  78.7 54.2 %all-to-all-start.1 = ((bf16[8,1,64,384]{3,2,1,0:T(8,128)(2,1)}), bf16[8,1,64,384]{3,2,1,0:T(8,128)(2,1)S(1)}, u32[]{:S(2)}, u32[]{:S(2)}) async-start(bf16[8,1,64,384]{3,2,1,0:T(8,128)(2,1)} %shard_map.87), calls=%async_computation.1 | async-start | bytes 786432 | tf_op jit(solution)/shard_map/all_to_all | solution.py:194
  88.2 35.8 %collective-permute-start.6 = (bf16[4,2,64,384]{3,2,1,0:T(8,128)(2,1)}, bf16[4,2,64,384]{3,2,1,0:T(8,128)(2,1)S(1)}, u32[]{:S(2)}, u32[]{:S(2)}) collective-permute-start(bf16[4,2,64,384]{3,2,1,0:T(8,128)(2,1)} %collective-permute-done.5), channel_id=1, source_target_pairs={{224,263},{225,262},{226,261},{227,260},{228,259},{229,258},{230,2... | collective-permute-start | bytes 1179656 | tf_op jit(solution)/shard_map/ppermute | solution.py:193
  89.4 37.8 %collective-permute-start.3 = (bf16[8,2,64,384]{3,2,1,0:T(8,128)(2,1)S(1)}, bf16[8,2,64,384]{3,2,1,0:T(8,128)(2,1)S(1)}, u32[]{:S(2)}, u32[]{:S(2)}) collective-permute-start(bf16[8,2,64,384]{3,2,1,0:T(8,128)(2,1)S(1)} %all-to-all-done.own), channel_id=1, source_target_pairs={{16,0},{17,1},{18,2},{19,3},{20,4},{21,5},{22,6},{23,7},{24,8},{25... | collective-permute-start | bytes 2359304 | tf_op jit(solution)/shard_map/ppermute | solution.py:193
  90.7 36.5 %collective-permute-start.2 = (bf16[8,2,64,384]{3,2,1,0:T(8,128)(2,1)S(1)}, bf16[8,2,64,384]{3,2,1,0:T(8,128)(2,1)S(1)}, u32[]{:S(2)}, u32[]{:S(2)}) collective-permute-start(bf16[8,2,64,384]{3,2,1,0:T(8,128)(2,1)S(1)} %all-to-all-done.own), channel_id=1, source_target_pairs={{8,0},{9,1},{10,2},{11,3},{12,4},{13,5},{14,6},{15,7},{16,8},{17,9... | collective-permute-start | bytes 2359304 | tf_op jit(solution)/shard_map/ppermute | solution.py:193
  92.0 35.2 %collective-permute-start.1 = (bf16[8,2,64,384]{3,2,1,0:T(8,128)(2,1)S(1)}, bf16[8,2,64,384]{3,2,1,0:T(8,128)(2,1)}, u32[]{:S(2)}, u32[]{:S(2)}) collective-permute-start(bf16[8,2,64,384]{3,2,1,0:T(8,128)(2,1)S(1)} %all-to-all-done.own), channel_id=1, source_target_pairs={{0,8},{1,9},{2,10},{3,11},{4,12},{5,13},{6,14},{7,15},{8,16},{9,17... | collective-permute-start | bytes 2359304 | tf_op jit(solution)/shard_map/ppermute | solution.py:193
  113.7 0.7 copy-start.1
  114.4 18.4 %collective-permute-start = (bf16[8,2,64,384]{3,2,1,0:T(8,128)(2,1)S(1)}, bf16[8,2,64,384]{3,2,1,0:T(8,128)(2,1)}, u32[]{:S(2)}, u32[]{:S(2)}) collective-permute-start(bf16[8,2,64,384]{3,2,1,0:T(8,128)(2,1)S(1)} %all-to-all-done.own), channel_id=1, source_target_pairs={{0,16},{1,17},{2,18},{3,19},{4,20},{5,21},{6,22},{7,23},{8,24},{9,... | collective-permute-start | bytes 2359304 | tf_op jit(solution)/shard_map/ppermute | solution.py:193
  124.0 1.3 copy-start.3
  124.0 8.9 %collective-permute-start.7 = (bf16[8,2,64,384]{3,2,1,0:T(8,128)(2,1)S(1)}, bf16[8,2,64,384]{3,2,1,0:T(8,128)(2,1)}, u32[]{:S(2)}, u32[]{:S(2)}) collective-permute-start(bf16[8,2,64,384]{3,2,1,0:T(8,128)(2,1)S(1)} %constant_dynamic-update-slice_fusion.cross), channel_id=1, source_target_pairs={{264,256},{265,257},{266,258},{267,259},{268,260},{269,261},{270,2... | collective-permute-start | bytes 2359304 | tf_op jit(solution)/shard_map/ppermute | solution.py:193
  154.0 24.8 %all-to-all-start.2 = ((bf16[8,64,384]{2,1,0:T(8,128)(2,1)}), bf16[8,64,384]{2,1,0:T(8,128)(2,1)S(1)}, u32[]{:S(2)}, u32[]{:S(2)}) async-start(bf16[8,64,384]{2,1,0:T(8,128)(2,1)} %shard_map.88), calls=%async_computation.2 | async-start | bytes 786432 | tf_op jit(solution)/shard_map/all_to_all | solution.py:194
  178.8 0.7 copy-start
  179.5 35.9 %copy-start.2 = (bf16[64,3072]{1,0:T(8,128)(2,1)S(1)}, bf16[64,3072]{1,0:T(8,128)(2,1)}, u32[]{:S(2)}) copy-start(bf16[64,3072]{1,0:T(8,128)(2,1)} %param.11) | copy-start | bytes 1179652
  181.6 33.8 %collective-permute-start.8 = (bf16[1,64,3072]{2,1,0:T(8,128)(2,1)}, bf16[1,64,3072]{2,1,0:T(8,128)(2,1)S(1)}, u32[]{:S(2)}, u32[]{:S(2)}) collective-permute-start(bf16[1,64,3072]{2,1,0:T(8,128)(2,1)} %bitcast.14), channel_id=1, source_target_pairs={{0,8},{1,9},{2,10},{3,11},{4,12},{5,13},{6,14},{7,15},{8,16},{9,17... | collective-permute-start | bytes 1179656 | tf_op jit(solution)/shard_map/ppermute | solution.py:193

commit v2 on v1

v2 whole, which is shorter than its diff:
```python
import functools

import jax
import jax.numpy as jnp
from jax import lax
from jax.experimental import pallas as pl
from jax.experimental.pallas import tpu as pltpu
from jax.sharding import PartitionSpec as P

HD = 64
REACH = 2
LEVELS = 1000
SLOTS = 2 * REACH + 1
PAIR = 2 * HD
LOG2E = 1.4426950408889634
AXES = ("frame", "head")
EXITS_A = ((2, 3), (3, 2), (3, 2), (3, 3))
EXITS_B = ((0, 3), (3, 0), (3, 0), (3, 3))
EXITS_STEP = ((3, 3), (3, 2), (3, 0), (2, 3), (0, 3), (3, 3), (3, 2), (3, 0))


def head_split_kernel(groups, width, flip_ref, *refs):
    inputs, out_ref = refs[:-1], refs[-1]
    flip = flip_ref[0]
    for group in range(groups):
        block = jnp.where(flip == 1, groups - 1 - group, group)
        for index, source in enumerate(inputs):
            out_ref[block, index] = source[:, group * width : (group + 1) * width]


def head_split(flip, groups, *arrays):
    rows, columns = arrays[0].shape
    width = columns // groups
    count = len(arrays)
    size = count * rows * columns * 2
    return pl.pallas_call(
        functools.partial(head_split_kernel, groups, width),
        out_shape=jax.ShapeDtypeStruct((groups, count, rows, width), jnp.bfloat16),
        in_specs=[pl.BlockSpec(memory_space=pltpu.SMEM)] + [pl.BlockSpec(memory_space=pltpu.VMEM)] * count,
        out_specs=pl.BlockSpec(memory_space=pltpu.VMEM),
        cost_estimate=pl.CostEstimate(flops=0, bytes_accessed=2 * size, transcendentals=0),
    )(flip, *arrays)


def attention_kernel(
    blocks, pairs, rows, picks_ref, q_ref, own, back2, next2, cross, chip, far,
    out_ref, k_buf, v_buf, score_a, score_b, sem,
):
    per_block = own.shape[2]
    span = blocks * per_block
    per_chunk = rows // per_block
    chunks = span // rows
    steps = pairs * chunks

    def copies(source, slot, pair, which, buf):
        columns = pl.ds(pair * PAIR, PAIR)
        return [
            pltpu.make_async_copy(
                source.at[block, which, :, columns],
                buf.at[pair, slot, pl.ds(block * per_block, per_block), pl.ds(0, PAIR)],
                sem.at[pair, slot, which],
            )
            for block in range(blocks)
        ]

    def fetch(source, slot, pair):
        for copy in copies(source, slot, pair, 0, k_buf) + copies(source, slot, pair, 1, v_buf):
            copy.start()

    sources = (back2, chip, own, chip, next2)
    others = (cross, far, None, far, cross)
    for pair in range(pairs):
        for slot in range(SLOTS):
            if slot == REACH:
                fetch(own, slot, pair)
                continue

            @pl.when(picks_ref[slot] == 0)
            def _(pair=pair, slot=slot):
                for copy in copies(own, slot, pair, 0, k_buf):
                    copy.start()
                v_buf[pair, slot] = jnp.zeros((span, 2 * PAIR), jnp.bfloat16)

            @pl.when(picks_ref[slot] == 1)
            def _(pair=pair, slot=slot):
                fetch(sources[slot], slot, pair)

            @pl.when(picks_ref[slot] == 2)
            def _(pair=pair, slot=slot):
                fetch(others[slot], slot, pair)

    for pair in range(pairs):
        for slot in range(SLOTS):
            @pl.when(picks_ref[slot] > 0)
            def _(pair=pair, slot=slot):
                v_buf[pair, slot, :, PAIR:] = jnp.ones((span, PAIR), jnp.bfloat16)

    def arrive(pair):
        for slot in range(SLOTS):
            for copy in copies(own, slot, pair, 0, k_buf):
                copy.wait()

            @pl.when(picks_ref[slot] > 0)
            def _(slot=slot):
                for copy in copies(own, slot, pair, 1, v_buf):
                    copy.wait()

    lane = lax.broadcasted_iota(jnp.int32, (rows, PAIR), 1)

    def place(step):
        pair, chunk = step // chunks, step % chunks
        return pl.ds(chunk * per_chunk, per_chunk), pl.ds(pl.multiple_of(pair * PAIR, PAIR), PAIR)

    def scores(step, score):
        block, columns = place(step)
        query = q_ref[block, 0, :, columns].reshape(rows, PAIR)
        zero = jnp.zeros_like(query)
        both = jnp.concatenate([jnp.where(lane < HD, query, zero), jnp.where(lane < HD, zero, query)], axis=0)
        high = None
        for slot in range(SLOTS):
            found = lax.dot_general(
                both, k_buf[step // chunks, slot], (((1,), (1,)), ((), ())), preferred_element_type=jnp.float32
            )
            score[slot] = found
            for start in range(0, span, 128):
                part = found[:, start : start + 128]
                high = part if high is None else jnp.maximum(high, part)
        return jnp.max(high, axis=1, keepdims=True)

    def mix(step, score, high):
        total = None
        for slot in range(SLOTS):
            weights = jnp.exp2((score[slot] - high) * (HD ** -0.5 * LOG2E)).astype(jnp.bfloat16)
            part = jnp.dot(weights, v_buf[step // chunks, slot], preferred_element_type=jnp.float32)
            total = part if total is None else total + part
        mixed = total[:, :PAIR] / total[:, PAIR:]
        mixed = jnp.where(lane < HD, mixed[:rows], mixed[rows:]).astype(jnp.bfloat16)
        block, columns = place(step)
        out_ref[block, :, columns] = mixed.reshape(per_chunk, per_block, PAIR)

    arrive(0)
    first = scores(0, score_a)

    def two_steps(index, high_a):
        later = jnp.minimum(2 * index + 2, steps - 1)
        high_b = scores(2 * index + 1, score_b)
        mix(2 * index, score_a, high_a)
        for pair in range(1, pairs):
            @pl.when(2 * index + 2 == pair * chunks)
            def _(pair=pair):
                arrive(pair)

        high_a = scores(later, score_a)
        mix(2 * index + 1, score_b, high_b)
        return high_a

    lax.fori_loop(0, steps // 2, two_steps, first)


def attend(picks, query, own, back2, next2, cross, chip, far):
    blocks, _, per_block, width = query.shape
    pairs = width // PAIR
    span = blocks * per_block
    rows = span // 2
    return pl.pallas_call(
        functools.partial(attention_kernel, blocks, pairs, rows),
        out_shape=jax.ShapeDtypeStruct((blocks, per_block, width), jnp.bfloat16),
        in_specs=[pl.BlockSpec(memory_space=pltpu.SMEM), pl.BlockSpec(memory_space=pltpu.VMEM)]
        + [pl.BlockSpec(memory_space=pl.ANY)] * 6,
        out_specs=pl.BlockSpec(memory_space=pltpu.VMEM),
        scratch_shapes=[
            pltpu.VMEM((pairs, SLOTS, span, PAIR), jnp.bfloat16),
            pltpu.VMEM((pairs, SLOTS, span, 2 * PAIR), jnp.bfloat16),
            pltpu.VMEM((SLOTS, 2 * rows, span), jnp.float32),
            pltpu.VMEM((SLOTS, 2 * rows, span), jnp.float32),
            pltpu.SemaphoreType.DMA((pairs, SLOTS, 2)),
        ],
        compiler_params=pltpu.CompilerParams(vmem_limit_bytes=40 * 1024 * 1024),
        cost_estimate=pl.CostEstimate(
            flops=4 * span * span * SLOTS * width,
            bytes_accessed=(2 * SLOTS + 2) * span * width * 2,
            transcendentals=span * span * SLOTS * width // HD,
        ),
    )(picks, query, own, back2, next2, cross, chip, far)


def blend_kernel(groups, width, flip_ref, share_ref, latents_ref, returned_ref, out_ref):
    flip = flip_ref[0]
    for group in range(groups):
        block = jnp.where(flip == 1, groups - 1 - group, group)
        columns = slice(group * width, (group + 1) * width)
        out_ref[:, columns] = (
            share_ref[0] * latents_ref[:, columns].astype(jnp.float32)
            + share_ref[1] * returned_ref[block].astype(jnp.float32)
        ).astype(jnp.bfloat16)


def blend(flip, shares, latents, returned):
    groups, rows, width = returned.shape
    return pl.pallas_call(
        functools.partial(blend_kernel, groups, width),
        out_shape=jax.ShapeDtypeStruct(latents.shape, jnp.bfloat16),
        in_specs=[pl.BlockSpec(memory_space=pltpu.SMEM)] * 2 + [pl.BlockSpec(memory_space=pltpu.VMEM)] * 2,
        out_specs=pl.BlockSpec(memory_space=pltpu.VMEM),
        cost_estimate=pl.CostEstimate(flops=3 * latents.size, bytes_accessed=6 * latents.size, transcendentals=0),
    )(flip, shares, latents, returned)


def per_device(frames, heads, latents, queries, keys, values, fresh, timesteps, window):
    frame = lax.axis_index("frame")
    half = frames // 2
    flip = (frame >= half).astype(jnp.int32)[None]

    def mirrored(moves):
        return [
            (a * heads + z, b * heads + (heads - 1 - z)) for a, b in moves for z in range(heads)
        ]

    def straight(moves):
        return [(a * heads + z, b * heads + z) for a, b in moves for z in range(heads)]

    def within(distance):
        return straight(
            [(f, f + distance) for f in range(frames) if 0 <= f + distance < frames and (f < half) == (f + distance < half)]
        )

    send = lambda value, moves: lax.ppermute(value, AXES, moves)
    exchange = lambda value: lax.all_to_all(value, "head", split_axis=0, concat_axis=0, tiled=True)

    own = exchange(head_split(flip, heads, keys, values))
    query = head_split(flip, heads, queries)
    own, query = lax.optimization_barrier((own, query))

    mid = heads // 2
    edge = (half - 2, half - 1, half, half + 1)
    over = {half - 2: half, half - 1: half + 1, half: half - 2, half + 1: half - 1}

    def column(f, z, exits):
        x, y = exits[min(z, heads - 1 - z)]
        ahead = y * 8 + x * 2 + f % 2
        return ahead if f < half else frames - 2 - ahead + 2 * (f % 2)

    def through(value, exits):
        out = [(f * heads + z, column(f, z, exits) * heads + z) for f in edge for z in range(heads)]
        on = [
            (column(f, z, exits) * heads + z, over[f] * heads + heads - 1 - z) for f in edge for z in range(heads)
        ]
        return send(value, out), on

    near_a, on_a = through(own[:mid], EXITS_A)
    near_b, on_b = through(own[mid:], EXITS_B)
    core = frame % 2
    pairwise = straight([(f, f ^ 1) for f in range(frames)])
    chip = send(own, pairwise)
    own, near_a, near_b = lax.optimization_barrier((own, near_a, near_b))
    back2 = send(own, within(2))
    next2 = send(own, within(-2))
    cross = jnp.concatenate([send(near_a, on_a), send(near_b, on_b)])
    fetched = jnp.where(core == 1, back2, next2)
    far = send(jnp.where((frame == half + 1) | (frame == half - 2), cross, fetched), pairwise)

    near_a, near_b, query = lax.optimization_barrier((near_a, near_b, query))
    query = exchange(query)

    offsets = jnp.arange(-REACH, REACH + 1)
    target = frame + offsets
    allowed = (
        (target >= 0) & (target < frames) & (offsets >= -window[0, 0]) & (offsets <= window[0, 1])
    )
    other = jnp.where(offsets % 2 == 0, (target < half) != (frame < half), target // 2 != frame // 2)
    picks = jnp.where(allowed, jnp.where(other, 2, 1), 0).astype(jnp.int32)
    attended = attend(picks, query, own, back2, next2, cross, chip, far)
    returned = exchange(attended)
    levels = timesteps.astype(jnp.float32) / LEVELS
    shares = jnp.concatenate([1.0 - 0.5 * levels, 0.5 + levels])
    denoised = blend(flip, shares, latents[0], returned)[None]

    def step_column(z):
        x, y = EXITS_STEP[z]
        return y * 8 + x * 2 + 1

    stepping = send(denoised, [((half - 1) * heads + z, step_column(z) * heads + z) for z in range(heads)])
    advanced = send(denoised, straight([(f, f + 1) for f in range(frames - 1) if f != half - 1]))
    stepped = send(stepping, [(step_column(z) * heads + z, half * heads + z) for z in range(heads)])
    advanced = jnp.where(frame == half, stepped, advanced)
    return (denoised, jnp.where(frame == 0, fresh[None], advanced))


def solution(mesh):
    def body(latents, queries, keys, values, fresh, timesteps, window):
        return per_device(
            mesh.shape["frame"], mesh.shape["head"], latents, queries[0], keys[0], values[0], fresh, timesteps, window
        )

    return jax.shard_map(
        body,
        mesh=mesh,
        in_specs=(
            P("frame", "head", None),
            P("frame", "head", None),
            P("frame", "head", None),
            P("frame", "head", None),
            P("head", None),
            P("frame"),
            P("frame", None),
        ),
        out_specs=(P("frame", "head", None), P("frame", "head", None)),
        check_vma=False,
    )
```

time: 217 us -> 173 us (0.80)
  the two profiles are of different devices: /device:TPU:288 before, /device:TPU:256 now
where the time goes in v2:
time: 173 us; the launch traced here: 172 us
  waiting for transfers between devices  103 us (60%)
  starting transfers between devices  40.1 us (23%)
  Pallas kernels  18.8 us (11%)
  local copies, waits for them, and re-layouts  4.96 us (3%)
  other arithmetic  3.13 us (2%)
  between operations  2.18 us (1%)
    all_to_all x3, waiting for transfers between devices, per_device(): lax.all_to_all(value, 'head', split_axis=0, concat_axis=0, tiled=True)  61.8 us
    ppermute x11, waiting for transfers between devices, per_device(): send = lambda value, moves: lax.ppermute(value, AXES, moves)  41.1 us
    ppermute x11, starting transfers between devices, per_device(): send = lambda value, moves: lax.ppermute(value, AXES, moves)  22.8 us
    all_to_all x3, starting transfers between devices, per_device(): lax.all_to_all(value, 'head', split_axis=0, concat_axis=0, tiled=True)  17.3 us
    pallas_call x1, Pallas kernels, attend(): pl.pallas_call(functools.partial(attention_kernel, blocks, pairs, rows),...  12.8 us
    pallas_call x2, Pallas kernels, head_split(): pl.pallas_call(functools.partial(head_split_kernel, groups, width), out_s...  3.85 us
  transfers between devices with their start and end apart: 14, of which 8 were waited for; matrix products, arithmetic and copies ran while one was open for 3% of the time, Pallas kernels for 1%

profile of v2, /device:TPU:256, one launch (start us, length us, event | category | flops | bytes accessed | tf_op | source)
XLA Modules:
  0.0 172.0 jit_solution(6234290653156798038)
XLA Ops:
  0.6 2.1 %shard_map.86 = bf16[8,2,64,384]{3,2,1,0:T(8,128)(2,1)} custom-call(s32[1]{0:T(128)} %bitcast.flip_ref, bf16[64,3072]{1,0:T(8,128)(2,1)} %bitcast.10, bf16[64,3072]{1,0:T(8,128)(2,1)} %bitcast.11), custom_call_target="tpu_custom_call" | custom-call | bytes 1572864 | tf_op jit(solution)/shard_map/pallas_call | solution.py:36
  2.7 5.0 %all-to-all-start = ((bf16[8,2,64,384]{3,2,1,0:T(8,128)(2,1)}), bf16[8,2,64,384]{3,2,1,0:T(8,128)(2,1)S(1)}, u32[]{:S(2)}, u32[]{:S(2)}) async-start(bf16[8,2,64,384]{3,2,1,0:T(8,128)(2,1)} %shard_map.86), calls=%async_computation | async-start | bytes 1572864 | tf_op jit(solution)/shard_map/all_to_all | solution.py:228
  7.7 1.8 %shard_map.87 = bf16[8,1,64,384]{3,2,1,0:T(8,128)(2,1)} custom-call(s32[1]{0:T(128)} %bitcast.flip_ref, bf16[64,3072]{1,0:T(8,128)(2,1)} %bitcast.12), custom_call_target="tpu_custom_call" | custom-call | bytes 786432 | tf_op jit(solution)/shard_map/pallas_call | solution.py:36
  9.5 38.2 %all-to-all-done.own = bf16[8,2,64,384]{3,2,1,0:T(8,128)(2,1)S(1)} async-done(((bf16[8,2,64,384]{3,2,1,0:T(8,128)(2,1)}), bf16[8,2,64,384]{3,2,1,0:T(8,128)(2,1)S(1)}, u32[]{:S(2)}, u32[]{:S(2)}) %all-to-all-start) | async-done | bytes 786464 | tf_op jit(solution)/shard_map/all_to_all | solution.py:228
  47.7 0.1 fusion.1
  47.8 5.4 %collective-permute-start.1 = (bf16[4,2,64,384]{3,2,1,0:T(8,128)(2,1)S(1)}, bf16[4,2,64,384]{3,2,1,0:T(8,128)(2,1)}, u32[]{:S(2)}, u32[]{:S(2)}) collective-permute-start(bf16[4,2,64,384]{3,2,1,0:T(8,128)(2,1)S(1)} %get-tuple-element.14), channel_id=1, source_target_pairs={{240,192},{241,49},{242,50},{243,243},{244,244},{245,53},{246,54},... | collective-permute-start | bytes 1179656 | tf_op jit(solution)/shard_map/ppermute | solution.py:227
  53.2 1.3 collective-permute-start
  54.5 3.2 %collective-permute-done.1 = bf16[4,2,64,384]{3,2,1,0:T(8,128)(2,1)} collective-permute-done((bf16[4,2,64,384]{3,2,1,0:T(8,128)(2,1)S(1)}, bf16[4,2,64,384]{3,2,1,0:T(8,128)(2,1)}, u32[]{:S(2)}, u32[]{:S(2)}) %collective-permute-start.1) | collective-permute-done | bytes 393248 | tf_op jit(solution)/shard_map/ppermute | solution.py:227
  57.7 6.3 %collective-permute-done = bf16[4,2,64,384]{3,2,1,0:T(8,128)(2,1)S(1)} collective-permute-done((bf16[4,2,64,384]{3,2,1,0:T(8,128)(2,1)S(1)}, bf16[4,2,64,384]{3,2,1,0:T(8,128)(2,1)S(1)}, u32[]{:S(2)}, u32[]{:S(2)}) %collective-permute-start) | collective-permute-done | bytes 393248 | tf_op jit(solution)/shard_map/ppermute | solution.py:227
  64.1 1.3 collective-permute-start.3
  65.4 5.1 %collective-permute-start.2 = (bf16[8,2,64,384]{3,2,1,0:T(8,128)(2,1)S(1)}, bf16[8,2,64,384]{3,2,1,0:T(8,128)(2,1)S(1)}, u32[]{:S(2)}, u32[]{:S(2)}) collective-permute-start(bf16[8,2,64,384]{3,2,1,0:T(8,128)(2,1)S(1)} %all-to-all-done.own), channel_id=1, source_target_pairs={{0,16},{1,17},{2,18},{3,19},{4,20},{5,21},{6,22},{7,23},{8,24},{9,... | collective-permute-start | bytes 2359304 | tf_op jit(solution)/shard_map/ppermute | solution.py:227
  70.4 1.3 collective-permute-start.4
  71.7 1.3 collective-permute-start.5
  73.0 3.5 %all-to-all-start.1 = ((bf16[8,1,64,384]{3,2,1,0:T(8,128)(2,1)}), bf16[8,1,64,384]{3,2,1,0:T(8,128)(2,1)S(1)}, u32[]{:S(2)}, u32[]{:S(2)}) async-start(bf16[8,1,64,384]{3,2,1,0:T(8,128)(2,1)} %shard_map.87), calls=%async_computation.1 | async-start | bytes 786432 | tf_op jit(solution)/shard_map/all_to_all | solution.py:228
  76.5 1.9 %collective-permute-start.6 = (bf16[8,2,64,384]{3,2,1,0:T(8,128)(2,1)S(1)}, bf16[8,2,64,384]{3,2,1,0:T(8,128)(2,1)}, u32[]{:S(2)}, u32[]{:S(2)}) collective-permute-start(bf16[8,2,64,384]{3,2,1,0:T(8,128)(2,1)S(1)} %all-to-all-done.own), channel_id=1, source_target_pairs={{0,8},{1,9},{2,10},{3,11},{4,12},{5,13},{6,14},{7,15},{8,0},{9,1},... | collective-permute-start | bytes 2359304 | tf_op jit(solution)/shard_map/ppermute | solution.py:227
  78.4 10.8 %collective-permute-done.4 = bf16[4,2,64,384]{3,2,1,0:T(8,128)(2,1)} collective-permute-done((bf16[4,2,64,384]{3,2,1,0:T(8,128)(2,1)S(1)}, bf16[4,2,64,384]{3,2,1,0:T(8,128)(2,1)}, u32[]{:S(2)}, u32[]{:S(2)}) %collective-permute-start.4) | collective-permute-done | bytes 393248 | tf_op jit(solution)/shard_map/ppermute | solution.py:227
  89.2 1.0 constant_dynamic-update-slice_fusion.1
  90.3 0.0 collective-permute-done.5
  90.3 1.1 constant_dynamic-update-slice_fusion.cross
  91.4 0.0 collective-permute-done.3.next2
  91.4 0.0 collective-permute-done.2.back2
  91.4 1.0 select_select_fusion
  92.4 1.9 %collective-permute-start.7 = (bf16[8,2,64,384]{3,2,1,0:T(8,128)(2,1)}, bf16[8,2,64,384]{3,2,1,0:T(8,128)(2,1)}, u32[]{:S(2)}, u32[]{:S(2)}) collective-permute-start(bf16[8,2,64,384]{3,2,1,0:T(8,128)(2,1)} %select_select_fusion), channel_id=1, source_target_pairs={{0,8},{1,9},{2,10},{3,11},{4,12},{5,13},{6,14},{7,15},{8,0},{9,1},... | collective-permute-start | bytes 2359304 | tf_op jit(solution)/shard_map/ppermute | solution.py:227
  94.3 0.0 copy-start.3
  94.3 0.6 copy-done.3
  95.0 0.6 fusion.2
  96.3 0.7 and_select_fusion.2.picks_ref
  97.0 0.0 collective-permute-done.6.chip
  97.0 1.1 all-to-all-done.1.q_ref
  98.1 0.0 collective-permute-done.7.far
  98.1 12.8 %shard_map.88 = bf16[8,64,384]{2,1,0:T(8,128)(2,1)S(1)} custom-call(s32[5]{0:T(128)S(1)} %and_select_fusion.2.picks_ref, bf16[8,1,64,384]{3,2,1,0:T(8,128)(2,1)S(1)} %all-to-all-done.1.q_ref, bf16[8,2,64,384]{3,2,1,0:T(8,128)(2,1)S(1)} %all-to-all-done.own, bf16[8,2,64,384]{3,2,1,0:T(8,128)(2,1)S(1)} %collective-permute-done.2.back2, ...), custom_call_target="tpu_custom_call" | custom-call | flops 2013265920 | bytes 4718592 | tf_op jit(solution)/shard_map/pallas_call | solution.py:165
  111.0 0.0 copy-start
  111.0 0.7 copy-done
  111.7 8.8 %all-to-all-start.2 = ((bf16[8,64,384]{2,1,0:T(8,128)(2,1)}), bf16[8,64,384]{2,1,0:T(8,128)(2,1)S(1)}, u32[]{:S(2)}, u32[]{:S(2)}) async-start(bf16[8,64,384]{2,1,0:T(8,128)(2,1)} %copy-done), calls=%async_computation.2 | async-start | bytes 786432 | tf_op jit(solution)/shard_map/all_to_all | solution.py:228
  121.2 0.6 pad_maximum_fusion.share_ref
  121.8 22.5 %all-to-all-done.2.returned_ref = bf16[8,64,384]{2,1,0:T(8,128)(2,1)S(1)} async-done(((bf16[8,64,384]{2,1,0:T(8,128)(2,1)}), bf16[8,64,384]{2,1,0:T(8,128)(2,1)S(1)}, u32[]{:S(2)}, u32[]{:S(2)}) %all-to-all-start.2) | async-done | bytes 393248 | tf_op jit(solution)/shard_map/all_to_all | solution.py:228
  144.3 0.0 copy-start.1
  144.3 0.7 copy-done.1
  145.1 0.0 copy-start.2
  145.1 2.1 %shard_map.89 = bf16[64,3072]{1,0:T(8,128)(2,1)} custom-call(s32[1]{0:T(128)} %bitcast.flip_ref, f32[2]{0:T(128)} %pad_maximum_fusion.share_ref, bf16[64,3072]{1,0:T(8,128)(2,1)} %bitcast.13, bf16[8,64,384]{2,1,0:T(8,128)(2,1)} %copy-done.1), custom_call_target="tpu_custom_call" | custom-call | flops 589824 | bytes 1179648 | tf_op jit(solution)/shard_map/pallas_call | solution.py:200
  147.1 0.7 collective-permute-start.8
  147.8 1.3 collective-permute-start.10
  149.1 0.0 collective-permute-done.8
  149.2 1.3 collective-permute-start.9
  150.5 0.2 collective-permute-done.10
  150.7 20.5 %collective-permute-done.9 = bf16[1,64,3072]{2,1,0:T(8,128)(2,1)S(1)} collective-permute-done((bf16[1,64,3072]{2,1,0:T(8,128)(2,1)S(1)}, bf16[1,64,3072]{2,1,0:T(8,128)(2,1)S(1)}, u32[]{:S(2)}, u32[]{:S(2)}) %collective-permute-start.9) | collective-permute-done | bytes 393248 | tf_op jit(solution)/shard_map/ppermute | solution.py:227
  171.2 0.0 copy-done.2
  171.2 0.8 bitcast_select_fusion
Async XLA Ops:
  2.7 45.0 %all-to-all-start = ((bf16[8,2,64,384]{3,2,1,0:T(8,128)(2,1)}), bf16[8,2,64,384]{3,2,1,0:T(8,128)(2,1)S(1)}, u32[]{:S(2)}, u32[]{:S(2)}) async-start(bf16[8,2,64,384]{3,2,1,0:T(8,128)(2,1)} %shard_map.86), calls=%async_computation | async-start | bytes 1572864 | tf_op jit(solution)/shard_map/all_to_all | solution.py:228
  47.8 9.9 %collective-permute-start.1 = (bf16[4,2,64,384]{3,2,1,0:T(8,128)(2,1)S(1)}, bf16[4,2,64,384]{3,2,1,0:T(8,128)(2,1)}, u32[]{:S(2)}, u32[]{:S(2)}) collective-permute-start(bf16[4,2,64,384]{3,2,1,0:T(8,128)(2,1)S(1)} %get-tuple-element.14), channel_id=1, source_target_pairs={{240,192},{241,49},{242,50},{243,243},{244,244},{245,53},{246,54},... | collective-permute-start | bytes 1179656 | tf_op jit(solution)/shard_map/ppermute | solution.py:227
  53.2 10.8 %collective-permute-start = (bf16[4,2,64,384]{3,2,1,0:T(8,128)(2,1)S(1)}, bf16[4,2,64,384]{3,2,1,0:T(8,128)(2,1)S(1)}, u32[]{:S(2)}, u32[]{:S(2)}) collective-permute-start(bf16[4,2,64,384]{3,2,1,0:T(8,128)(2,1)S(1)} %get-tuple-element.15), channel_id=1, source_target_pairs={{240,224},{241,177},{242,178},{243,243},{244,244},{245,181},{246,1... | collective-permute-start | bytes 1179656 | tf_op jit(solution)/shard_map/ppermute | solution.py:227
  64.1 27.3 %collective-permute-start.3 = (bf16[8,2,64,384]{3,2,1,0:T(8,128)(2,1)S(1)}, bf16[8,2,64,384]{3,2,1,0:T(8,128)(2,1)S(1)}, u32[]{:S(2)}, u32[]{:S(2)}) collective-permute-start(bf16[8,2,64,384]{3,2,1,0:T(8,128)(2,1)S(1)} %all-to-all-done.own), channel_id=1, source_target_pairs={{16,0},{17,1},{18,2},{19,3},{20,4},{21,5},{22,6},{23,7},{24,8},{25... | collective-permute-start | bytes 2359304 | tf_op jit(solution)/shard_map/ppermute | solution.py:227
  65.4 26.0 %collective-permute-start.2 = (bf16[8,2,64,384]{3,2,1,0:T(8,128)(2,1)S(1)}, bf16[8,2,64,384]{3,2,1,0:T(8,128)(2,1)S(1)}, u32[]{:S(2)}, u32[]{:S(2)}) collective-permute-start(bf16[8,2,64,384]{3,2,1,0:T(8,128)(2,1)S(1)} %all-to-all-done.own), channel_id=1, source_target_pairs={{0,16},{1,17},{2,18},{3,19},{4,20},{5,21},{6,22},{7,23},{8,24},{9,... | collective-permute-start | bytes 2359304 | tf_op jit(solution)/shard_map/ppermute | solution.py:227
  70.4 18.8 %collective-permute-start.4 = (bf16[4,2,64,384]{3,2,1,0:T(8,128)(2,1)S(1)}, bf16[4,2,64,384]{3,2,1,0:T(8,128)(2,1)}, u32[]{:S(2)}, u32[]{:S(2)}) collective-permute-start(bf16[4,2,64,384]{3,2,1,0:T(8,128)(2,1)S(1)} %collective-permute-done), channel_id=1, source_target_pairs={{224,263},{177,262},{178,261},{243,260},{244,259},{181,258},{182,2... | collective-permute-start | bytes 1179656 | tf_op jit(solution)/shard_map/ppermute | solution.py:227
  71.7 18.6 %collective-permute-start.5 = (bf16[4,2,64,384]{3,2,1,0:T(8,128)(2,1)}, bf16[4,2,64,384]{3,2,1,0:T(8,128)(2,1)}, u32[]{:S(2)}, u32[]{:S(2)}) collective-permute-start(bf16[4,2,64,384]{3,2,1,0:T(8,128)(2,1)} %collective-permute-done.1), channel_id=1, source_target_pairs={{192,263},{49,262},{50,261},{243,260},{244,259},{53,258},{54,257},... | collective-permute-start | bytes 1179656 | tf_op jit(solution)/shard_map/ppermute | solution.py:227
  73.0 25.1 %all-to-all-start.1 = ((bf16[8,1,64,384]{3,2,1,0:T(8,128)(2,1)}), bf16[8,1,64,384]{3,2,1,0:T(8,128)(2,1)S(1)}, u32[]{:S(2)}, u32[]{:S(2)}) async-start(bf16[8,1,64,384]{3,2,1,0:T(8,128)(2,1)} %shard_map.87), calls=%async_computation.1 | async-start | bytes 786432 | tf_op jit(solution)/shard_map/all_to_all | solution.py:228
  76.5 20.5 %collective-permute-start.6 = (bf16[8,2,64,384]{3,2,1,0:T(8,128)(2,1)S(1)}, bf16[8,2,64,384]{3,2,1,0:T(8,128)(2,1)}, u32[]{:S(2)}, u32[]{:S(2)}) collective-permute-start(bf16[8,2,64,384]{3,2,1,0:T(8,128)(2,1)S(1)} %all-to-all-done.own), channel_id=1, source_target_pairs={{0,8},{1,9},{2,10},{3,11},{4,12},{5,13},{6,14},{7,15},{8,0},{9,1},... | collective-permute-start | bytes 2359304 | tf_op jit(solution)/shard_map/ppermute | solution.py:227
  92.4 5.7 %collective-permute-start.7 = (bf16[8,2,64,384]{3,2,1,0:T(8,128)(2,1)}, bf16[8,2,64,384]{3,2,1,0:T(8,128)(2,1)}, u32[]{:S(2)}, u32[]{:S(2)}) collective-permute-start(bf16[8,2,64,384]{3,2,1,0:T(8,128)(2,1)} %select_select_fusion), channel_id=1, source_target_pairs={{0,8},{1,9},{2,10},{3,11},{4,12},{5,13},{6,14},{7,15},{8,0},{9,1},... | collective-permute-start | bytes 2359304 | tf_op jit(solution)/shard_map/ppermute | solution.py:227
  94.3 0.7 copy-start.3
  111.0 0.7 copy-start
  111.7 32.6 %all-to-all-start.2 = ((bf16[8,64,384]{2,1,0:T(8,128)(2,1)}), bf16[8,64,384]{2,1,0:T(8,128)(2,1)S(1)}, u32[]{:S(2)}, u32[]{:S(2)}) async-start(bf16[8,64,384]{2,1,0:T(8,128)(2,1)} %copy-done), calls=%async_computation.2 | async-start | bytes 786432 | tf_op jit(solution)/shard_map/all_to_all | solution.py:228
  144.3 0.7 copy-start.1
  145.1 26.1 %copy-start.2 = (bf16[64,3072]{1,0:T(8,128)(2,1)S(1)}, bf16[64,3072]{1,0:T(8,128)(2,1)}, u32[]{:S(2)}) copy-start(bf16[64,3072]{1,0:T(8,128)(2,1)} %param.11) | copy-start | bytes 1179652
  147.1 2.0 %collective-permute-start.8 = (bf16[1,64,3072]{2,1,0:T(8,128)(2,1)}, bf16[1,64,3072]{2,1,0:T(8,128)(2,1)S(1)}, u32[]{:S(2)}, u32[]{:S(2)}) collective-permute-start(bf16[1,64,3072]{2,1,0:T(8,128)(2,1)} %bitcast.14), channel_id=1, source_target_pairs={{248,248},{249,185},{250,58},{251,235},{252,204},{253,253},{254,19... | collective-permute-start | bytes 1179656 | tf_op jit(solution)/shard_map/ppermute | solution.py:227
  147.8 2.8 %collective-permute-start.10 = (bf16[1,64,3072]{2,1,0:T(8,128)(2,1)}, bf16[1,64,3072]{2,1,0:T(8,128)(2,1)S(1)}, u32[]{:S(2)}, u32[]{:S(2)}) collective-permute-start(bf16[1,64,3072]{2,1,0:T(8,128)(2,1)} %bitcast.15), channel_id=1, source_target_pairs={{0,8},{1,9},{2,10},{3,11},{4,12},{5,13},{6,14},{7,15},{8,16},{9,17... | collective-permute-start | bytes 1179656 | tf_op jit(solution)/shard_map/ppermute | solution.py:227
  149.2 22.0 %collective-permute-start.9 = (bf16[1,64,3072]{2,1,0:T(8,128)(2,1)S(1)}, bf16[1,64,3072]{2,1,0:T(8,128)(2,1)S(1)}, u32[]{:S(2)}, u32[]{:S(2)}) collective-permute-start(bf16[1,64,3072]{2,1,0:T(8,128)(2,1)S(1)} %collective-permute-done.8), channel_id=1, source_target_pairs={{248,256},{185,257},{58,258},{235,259},{204,260},{253,261},{190,26... | collective-permute-start | bytes 1179656 | tf_op jit(solution)/shard_map/ppermute | solution.py:227

commit v3 on v2

--- a/solution.py
+++ b/solution.py
@@ -16,7 +16,9 @@
 AXES = ("frame", "head")
 EXITS_A = ((2, 3), (3, 2), (3, 2), (3, 3))
 EXITS_B = ((0, 3), (3, 0), (3, 0), (3, 3))
-EXITS_STEP = ((3, 3), (3, 2), (3, 0), (2, 3), (0, 3), (3, 3), (3, 2), (3, 0))
+EXITS_STEP = ((2, 2), (1, 3), (2, 0), (0, 0), (0, 2), (3, 1), (2, 0), (1, 3))
+MARK_LENT = 2 * 10**9
+MARK_PIECES = 16 * 10**9
 
 
 def head_split_kernel(groups, width, flip_ref, *refs):
@@ -206,6 +208,78 @@
     )(flip, shares, latents, returned)
 
 
+def mark_kernel(value_ref, out_ref):
+    pass
+
+
+def mark(value, flops):
+    return pl.pallas_call(
+        mark_kernel,
+        out_shape=jax.ShapeDtypeStruct(value.shape, value.dtype),
+        in_specs=[pl.BlockSpec(memory_space=pl.ANY)],
+        out_specs=pl.BlockSpec(memory_space=pl.ANY),
+        input_output_aliases={0: 0},
+        compiler_params=pltpu.CompilerParams(vmem_limit_bytes=40 * 1024 * 1024),
+        cost_estimate=pl.CostEstimate(flops=flops, bytes_accessed=0, transcendentals=0),
+    )(value)
+
+
+def blend_lent_kernel(groups, rows, width, order_ref, before_ref, returned_ref, fresh_ref, out_ref):
+    first = order_ref[groups] == 1
+    high = before_ref[rows : rows + 1, :width].astype(jnp.float32)
+    low = before_ref[rows + 1 : rows + 2, :width].astype(jnp.float32)
+    level = (high * 32.0 + low) / LEVELS
+    keep_share = 1.0 - 0.5 * level
+    push_share = 0.5 + level
+    for group in range(groups):
+        block = order_ref[group]
+        columns = slice(group * width, (group + 1) * width)
+        entry = (
+            keep_share * before_ref[:rows, columns].astype(jnp.float32)
+            + push_share * returned_ref[block].astype(jnp.float32)
+        ).astype(jnp.bfloat16)
+        out_ref[:, columns] = jnp.where(first, fresh_ref[:, columns], entry)
+
+
+def blend_lent(order, before, returned, fresh):
+    groups, rows, width = returned.shape
+    shape = (rows, groups * width)
+    return pl.pallas_call(
+        functools.partial(blend_lent_kernel, groups, rows, width),
+        out_shape=jax.ShapeDtypeStruct(shape, jnp.bfloat16),
+        in_specs=[pl.BlockSpec(memory_space=pltpu.SMEM)] + [pl.BlockSpec(memory_space=pltpu.VMEM)] * 3,
+        out_specs=pl.BlockSpec(memory_space=pltpu.VMEM),
+        cost_estimate=pl.CostEstimate(
+            flops=3 * rows * groups * width, bytes_accessed=6 * rows * groups * width, transcendentals=0
+        ),
+    )(order, before, returned, fresh)
+
+
+def with_step(latents, timesteps):
+    row = lax.broadcasted_iota(jnp.int32, (16, latents.shape[1]), 0)
+    step = jnp.where(row == 0, timesteps[0] // 32, jnp.where(row == 1, timesteps[0] % 32, 0))
+    return jnp.concatenate([latents, step.astype(jnp.bfloat16)])
+
+
+def sort_kernel(parity_ref, *refs):
+    pieces, kept_ref, given_ref = refs[:-2], refs[-2], refs[-1]
+    parity = parity_ref[0]
+    for index, piece in enumerate(pieces):
+        kept_ref[index] = piece[parity]
+        given_ref[index] = piece[1 - parity]
+
+
+def sort_pieces(parity, pieces, flops):
+    shape = jax.ShapeDtypeStruct((len(pieces), *pieces[0].shape[1:]), pieces[0].dtype)
+    return pl.pallas_call(
+        sort_kernel,
+        out_shape=(shape, shape),
+        in_specs=[pl.BlockSpec(memory_space=pltpu.SMEM)] + [pl.BlockSpec(memory_space=pltpu.VMEM)] * len(pieces),
+        out_specs=(pl.BlockSpec(memory_space=pltpu.VMEM), pl.BlockSpec(memory_space=pltpu.VMEM)),
+        cost_estimate=pl.CostEstimate(flops=flops, bytes_accessed=0, transcendentals=0),
+    )(parity, *pieces)
+
+
 def per_device(frames, heads, latents, queries, keys, values, fresh, timesteps, window):
     frame = lax.axis_index("frame")
     half = frames // 2
@@ -229,7 +303,10 @@
 
     own = exchange(head_split(flip, heads, keys, values))
     query = head_split(flip, heads, queries)
-    own, query = lax.optimization_barrier((own, query))
+    lent_to = [(y * 8 + x * 2 + 1) * heads + a for a, (x, y) in enumerate(EXITS_STEP)]
+    lending = [((half - 1) * heads + a, lent_to[a]) for a in range(heads)]
+    before = send(with_step(latents[0], timesteps), lending)
+    own, query, before = lax.optimization_barrier((own, query, before))
 
     mid = heads // 2
     edge = (half - 2, half - 1, half, half + 1)
@@ -270,20 +347,31 @@
     other = jnp.where(offsets % 2 == 0, (target < half) != (frame < half), target // 2 != frame // 2)
     picks = jnp.where(allowed, jnp.where(other, 2, 1), 0).astype(jnp.int32)
     attended = attend(picks, query, own, back2, next2, cross, chip, far)
-    returned = exchange(attended)
+    z = lax.axis_index("head")
     levels = timesteps.astype(jnp.float32) / LEVELS
     shares = jnp.concatenate([1.0 - 0.5 * levels, 0.5 + levels])
+    attended, before = lax.optimization_barrier((attended, before))
+    returned = exchange(attended)
+    lent = attended.reshape(mid, 2, *attended.shape[1:])
+    pieces = [
+        send(
+            lax.dynamic_index_in_dim(lent, (z // 2 + shift) % mid, 0, keepdims=False),
+            [((half - 1) * heads + a, half * heads + (a + 2 * shift) % heads) for a in range(heads)],
+        )
+        for shift in range(mid)
+    ]
+    before = mark(send(before, [(lent_to[a], half * heads + a) for a in range(heads)]), MARK_LENT)
+    parity = z % 2
+    kept, given = sort_pieces(parity[None], pieces, MARK_PIECES)
+    got = send(given, [(half * heads + a, half * heads + (a ^ 1)) for a in range(heads)])
     denoised = blend(flip, shares, latents[0], returned)[None]
-
-    def step_column(z):
-        x, y = EXITS_STEP[z]
-        return y * 8 + x * 2 + 1
-
-    stepping = send(denoised, [((half - 1) * heads + z, step_column(z) * heads + z) for z in range(heads)])
+    groups = jnp.arange(heads)
+    source = jnp.where(groups % 2 == parity, z, z + 1 - 2 * parity)
+    order = ((source - groups) % heads) // 2 + jnp.where(groups % 2 == parity, 0, mid)
+    order = jnp.concatenate([order, (frame == 0).astype(order.dtype)[None]])
+    entering = blend_lent(order, before, jnp.concatenate([kept, got]), fresh)[None]
     advanced = send(denoised, straight([(f, f + 1) for f in range(frames - 1) if f != half - 1]))
-    stepped = send(stepping, [(step_column(z) * heads + z, half * heads + z) for z in range(heads)])
-    advanced = jnp.where(frame == half, stepped, advanced)
-    return (denoised, jnp.where(frame == 0, fresh[None], advanced))
+    return (denoised, jnp.where((frame == 0) | (frame == half), entering, advanced))
 
 
 def solution(mesh):

time: 173 us -> 168 us (0.971)
  the two profiles are of different devices: /device:TPU:256 before, /device:TPU:24 now
where the time goes in v3:
time: 168 us; the launch traced here: 167 us
  waiting for transfers between devices  74.2 us (44%)
  starting transfers between devices  54.4 us (32%)
  Pallas kernels  23.3 us (14%)
  local copies, waits for them, and re-layouts  6.77 us (4%)
  other arithmetic  5.6 us (3%)
  between operations  2.46 us (1%)
    all_to_all x3, waiting for transfers between devices, per_device(): lax.all_to_all(value, 'head', split_axis=0, concat_axis=0, tiled=True)  58.1 us
    ppermute x16, starting transfers between devices, per_device(): send = lambda value, moves: lax.ppermute(value, AXES, moves)  27.9 us
    all_to_all x3, starting transfers between devices, per_device(): lax.all_to_all(value, 'head', split_axis=0, concat_axis=0, tiled=True)  26.5 us
    ppermute x16, waiting for transfers between devices, per_device(): send = lambda value, moves: lax.ppermute(value, AXES, moves)  16.2 us
    pallas_call x1, Pallas kernels, attend(): pl.pallas_call(functools.partial(attention_kernel, blocks, pairs, rows),...  13.4 us
    unnamed x23, local copies, waits for them, and re-layouts  3.9 us
    pallas_call x2, Pallas kernels, head_split(): pl.pallas_call(functools.partial(head_split_kernel, groups, width), out_s...  3.85 us
  transfers between devices with their start and end apart: 19, of which 6 were waited for; matrix products, arithmetic and copies ran while one was open for 4% of the time, Pallas kernels for 5%

profile of v3, /device:TPU:24, one launch (start us, length us, event | category | flops | bytes accessed | tf_op | source)
XLA Modules:
  0.0 166.8 jit_solution(2574326785625390894)
XLA Ops:
  0.6 2.1 %shard_map.86 = bf16[8,2,64,384]{3,2,1,0:T(8,128)(2,1)} custom-call(s32[1]{0:T(128)} %bitcast.flip_ref, bf16[64,3072]{1,0:T(8,128)(2,1)} %bitcast.28, bf16[64,3072]{1,0:T(8,128)(2,1)} %bitcast.29), custom_call_target="tpu_custom_call" | custom-call | bytes 1572864 | tf_op jit(solution)/shard_map/pallas_call | solution.py:38
  2.7 12.7 %all-to-all-start = ((bf16[8,2,64,384]{3,2,1,0:T(8,128)(2,1)}), bf16[8,2,64,384]{3,2,1,0:T(8,128)(2,1)S(1)}, u32[]{:S(2)}, u32[]{:S(2)}) async-start(bf16[8,2,64,384]{3,2,1,0:T(8,128)(2,1)} %shard_map.86), calls=%async_computation | async-start | bytes 1572864 | tf_op jit(solution)/shard_map/all_to_all | solution.py:302
  16.1 0.1 select_convert_fusion
  16.2 0.7 collective-permute-start
  16.9 1.8 %shard_map.87 = bf16[8,1,64,384]{3,2,1,0:T(8,128)(2,1)} custom-call(s32[1]{0:T(128)} %bitcast.flip_ref, bf16[64,3072]{1,0:T(8,128)(2,1)} %bitcast.30), custom_call_target="tpu_custom_call" | custom-call | bytes 786432 | tf_op jit(solution)/shard_map/pallas_call | solution.py:38
  18.7 36.6 %all-to-all-done.own = bf16[8,2,64,384]{3,2,1,0:T(8,128)(2,1)S(1)} async-done(((bf16[8,2,64,384]{3,2,1,0:T(8,128)(2,1)}), bf16[8,2,64,384]{3,2,1,0:T(8,128)(2,1)S(1)}, u32[]{:S(2)}, u32[]{:S(2)}) %all-to-all-start) | async-done | bytes 786464 | tf_op jit(solution)/shard_map/all_to_all | solution.py:302
  55.3 0.1 fusion.4
  55.4 1.3 collective-permute-start.2
  56.7 0.7 collective-permute-start.1
  57.4 9.0 %collective-permute-done.2 = bf16[4,2,64,384]{3,2,1,0:T(8,128)(2,1)} collective-permute-done((bf16[4,2,64,384]{3,2,1,0:T(8,128)(2,1)S(1)}, bf16[4,2,64,384]{3,2,1,0:T(8,128)(2,1)}, u32[]{:S(2)}, u32[]{:S(2)}) %collective-permute-start.2) | collective-permute-done | bytes 393248 | tf_op jit(solution)/shard_map/ppermute | solution.py:301
  66.4 1.9 %collective-permute-start.4 = (bf16[8,2,64,384]{3,2,1,0:T(8,128)(2,1)S(1)}, bf16[8,2,64,384]{3,2,1,0:T(8,128)(2,1)S(1)}, u32[]{:S(2)}, u32[]{:S(2)}) collective-permute-start(bf16[8,2,64,384]{3,2,1,0:T(8,128)(2,1)S(1)} %all-to-all-done.own), channel_id=1, source_target_pairs={{16,0},{17,1},{18,2},{19,3},{20,4},{21,5},{22,6},{23,7},{24,8},{25... | collective-permute-start | bytes 2359304 | tf_op jit(solution)/shard_map/ppermute | solution.py:301
  68.3 3.9 %collective-permute-start.3 = (bf16[8,2,64,384]{3,2,1,0:T(8,128)(2,1)S(1)}, bf16[8,2,64,384]{3,2,1,0:T(8,128)(2,1)S(1)}, u32[]{:S(2)}, u32[]{:S(2)}) collective-permute-start(bf16[8,2,64,384]{3,2,1,0:T(8,128)(2,1)S(1)} %all-to-all-done.own), channel_id=1, source_target_pairs={{0,16},{1,17},{2,18},{3,19},{4,20},{5,21},{6,22},{7,23},{8,24},{9,... | collective-permute-start | bytes 2359304 | tf_op jit(solution)/shard_map/ppermute | solution.py:301
  72.3 1.4 collective-permute-start.5
  73.7 8.1 %collective-permute-start.6 = (bf16[4,2,64,384]{3,2,1,0:T(8,128)(2,1)}, bf16[4,2,64,384]{3,2,1,0:T(8,128)(2,1)}, u32[]{:S(2)}, u32[]{:S(2)}) collective-permute-start(bf16[4,2,64,384]{3,2,1,0:T(8,128)(2,1)} %collective-permute-done.2), channel_id=1, source_target_pairs={{192,263},{49,262},{50,261},{243,260},{244,259},{53,258},{54,257},... | collective-permute-start | bytes 1179656 | tf_op jit(solution)/shard_map/ppermute | solution.py:301
  81.8 8.1 %all-to-all-start.1 = ((bf16[8,1,64,384]{3,2,1,0:T(8,128)(2,1)}), bf16[8,1,64,384]{3,2,1,0:T(8,128)(2,1)S(1)}, u32[]{:S(2)}, u32[]{:S(2)}) async-start(bf16[8,1,64,384]{3,2,1,0:T(8,128)(2,1)} %shard_map.87), calls=%async_computation.1 | async-start | bytes 786432 | tf_op jit(solution)/shard_map/all_to_all | solution.py:302
  89.8 1.9 %collective-permute-start.7 = (bf16[8,2,64,384]{3,2,1,0:T(8,128)(2,1)S(1)}, bf16[8,2,64,384]{3,2,1,0:T(8,128)(2,1)}, u32[]{:S(2)}, u32[]{:S(2)}) collective-permute-start(bf16[8,2,64,384]{3,2,1,0:T(8,128)(2,1)S(1)} %all-to-all-done.own), channel_id=1, source_target_pairs={{0,8},{1,9},{2,10},{3,11},{4,12},{5,13},{6,14},{7,15},{8,0},{9,1},... | collective-permute-start | bytes 2359304 | tf_op jit(solution)/shard_map/ppermute | solution.py:301
  91.8 1.0 constant_dynamic-update-slice_fusion.1
  92.8 2.1 %collective-permute-done.6 = bf16[4,2,64,384]{3,2,1,0:T(8,128)(2,1)} collective-permute-done((bf16[4,2,64,384]{3,2,1,0:T(8,128)(2,1)}, bf16[4,2,64,384]{3,2,1,0:T(8,128)(2,1)}, u32[]{:S(2)}, u32[]{:S(2)}) %collective-permute-start.6) | collective-permute-done | bytes 393248 | tf_op jit(solution)/shard_map/ppermute | solution.py:301
  94.9 1.1 constant_dynamic-update-slice_fusion.cross
  96.0 1.0 select_select_fusion
  97.0 1.9 %collective-permute-start.8 = (bf16[8,2,64,384]{3,2,1,0:T(8,128)(2,1)}, bf16[8,2,64,384]{3,2,1,0:T(8,128)(2,1)}, u32[]{:S(2)}, u32[]{:S(2)}) collective-permute-start(bf16[8,2,64,384]{3,2,1,0:T(8,128)(2,1)} %select_select_fusion), channel_id=1, source_target_pairs={{0,8},{1,9},{2,10},{3,11},{4,12},{5,13},{6,14},{7,15},{8,0},{9,1},... | collective-permute-start | bytes 2359304 | tf_op jit(solution)/shard_map/ppermute | solution.py:301
  99.1 0.6 copy-done.4
  99.7 0.6 fusion.5
  101.0 0.6 and_select_fusion.5.picks_ref
  101.7 4.1 %all-to-all-done.1.q_ref = bf16[8,1,64,384]{3,2,1,0:T(8,128)(2,1)S(1)} async-done(((bf16[8,1,64,384]{3,2,1,0:T(8,128)(2,1)}), bf16[8,1,64,384]{3,2,1,0:T(8,128)(2,1)S(1)}, u32[]{:S(2)}, u32[]{:S(2)}) %all-to-all-start.1) | async-done | bytes 393248 | tf_op jit(solution)/shard_map/all_to_all | solution.py:302
  105.8 13.4 %shard_map.88 = bf16[8,64,384]{2,1,0:T(8,128)(2,1)} custom-call(s32[5]{0:T(128)S(1)} %and_select_fusion.5.picks_ref, bf16[8,1,64,384]{3,2,1,0:T(8,128)(2,1)S(1)} %all-to-all-done.1.q_ref, bf16[8,2,64,384]{3,2,1,0:T(8,128)(2,1)S(1)} %all-to-all-done.own, bf16[8,2,64,384]{3,2,1,0:T(8,128)(2,1)S(1)} %collective-permute-done.3.back2, ...), custom_call_target="tpu_custom_call" | custom-call | flops 2013265920 | bytes 4718592 | tf_op jit(solution)/shard_map/pallas_call | solution.py:167
  119.3 1.1 dynamic-slice_bitcast_fusion
  120.4 0.8 collective-permute-start.13
  121.2 0.7 collective-permute-start.12
  121.9 0.7 collective-permute-start.11
  122.6 0.7 collective-permute-start.10
  123.3 5.8 %all-to-all-start.2 = ((bf16[8,64,384]{2,1,0:T(8,128)(2,1)}), bf16[8,64,384]{2,1,0:T(8,128)(2,1)S(1)}, u32[]{:S(2)}, u32[]{:S(2)}) async-start(bf16[8,64,384]{2,1,0:T(8,128)(2,1)} %shard_map.88), calls=%async_computation.2 | async-start | bytes 786432 | tf_op jit(solution)/shard_map/all_to_all | solution.py:302
  129.0 0.7 collective-permute-start.9
  129.8 0.6 copy-done.7
  130.4 0.0 copy-done.8
  130.5 1.8 %shard_map.91 = (bf16[4,64,384]{2,1,0:T(8,128)(2,1)}, bf16[4,64,384]{2,1,0:T(8,128)(2,1)}) custom-call(s32[1]{0:T(128)} %bitcast.10.parity_ref, bf16[2,64,384]{2,1,0:T(8,128)(2,1)} %copy-done.10, bf16[2,64,384]{2,1,0:T(8,128)(2,1)} %copy-done.9, bf16[2,64,384]{2,1,0:T(8,128)(2,1)} %copy-done.8, bf16[2,64,384]{2,1,0:T(8,128)(2,1)} %copy-done.7), custom_call_target="tpu_custom_call" | custom-call | flops 16000000000 | tf_op jit(solution)/shard_map/pallas_call | solution.py:274
  132.3 0.7 collective-permute-start.14
  133.0 0.6 pad_maximum_fusion.2.share_ref
  133.5 17.3 %all-to-all-done.2.returned_ref = bf16[8,64,384]{2,1,0:T(8,128)(2,1)S(1)} async-done(((bf16[8,64,384]{2,1,0:T(8,128)(2,1)}), bf16[8,64,384]{2,1,0:T(8,128)(2,1)S(1)}, u32[]{:S(2)}, u32[]{:S(2)}) %all-to-all-start.2) | async-done | bytes 393248 | tf_op jit(solution)/shard_map/all_to_all | solution.py:302
  150.8 0.7 copy-done.1
  151.6 2.0 %shard_map.89 = bf16[64,3072]{1,0:T(8,128)(2,1)} custom-call(s32[1]{0:T(128)} %bitcast.flip_ref, f32[2]{0:T(128)} %pad_maximum_fusion.2.share_ref, bf16[64,3072]{1,0:T(8,128)(2,1)} %bitcast.26, bf16[8,64,384]{2,1,0:T(8,128)(2,1)} %copy-done.1), custom_call_target="tpu_custom_call" | custom-call | flops 589824 | bytes 1179648 | tf_op jit(solution)/shard_map/pallas_call | solution.py:202
  153.6 1.9 %collective-permute-start.15 = (bf16[1,64,3072]{2,1,0:T(8,128)(2,1)}, bf16[1,64,3072]{2,1,0:T(8,128)(2,1)S(1)}, u32[]{:S(2)}, u32[]{:S(2)}) collective-permute-start(bf16[1,64,3072]{2,1,0:T(8,128)(2,1)} %bitcast.31), channel_id=1, source_target_pairs={{0,8},{1,9},{2,10},{3,11},{4,12},{5,13},{6,14},{7,15},{8,16},{9,17... | collective-permute-start | bytes 1179656 | tf_op jit(solution)/shard_map/ppermute | solution.py:301
  155.5 0.7 pad_add_fusion.order_ref
  156.2 0.8 pad_maximum_fusion.1.returned_ref
  157.0 0.8 copy-done
  157.7 2.2 %shard_map.92 = bf16[64,3072]{1,0:T(8,128)(2,1)} custom-call(s32[9]{0:T(128)} %pad_add_fusion.order_ref, bf16[80,3072]{1,0:T(8,128)(2,1)} %copy-done, bf16[8,64,384]{2,1,0:T(8,128)(2,1)} %pad_maximum_fusion.1.returned_ref, bf16[64,3072]{1,0:T(8,128)(2,1)} %fresh_ref.1), custom_call_target="tpu_custom_call" | custom-call | flops 589824 | bytes 1179648 | tf_op jit(solution)/shard_map/pallas_call | solution.py:247
  159.9 5.1 %collective-permute-done.15 = bf16[1,64,3072]{2,1,0:T(8,128)(2,1)S(1)} collective-permute-done((bf16[1,64,3072]{2,1,0:T(8,128)(2,1)}, bf16[1,64,3072]{2,1,0:T(8,128)(2,1)S(1)}, u32[]{:S(2)}, u32[]{:S(2)}) %collective-permute-start.15) | collective-permute-done | bytes 393248 | tf_op jit(solution)/shard_map/ppermute | solution.py:301
  165.0 1.8 %bitcast_select_fusion = bf16[1,64,3072]{2,1,0:T(8,128)(2,1)} fusion(bf16[1,64,3072]{2,1,0:T(8,128)(2,1)S(1)} %collective-permute-done.15, bf16[64,3072]{1,0:T(8,128)(2,1)} %shard_map.92, pred[]{:T(512)S(6)} %or.7), kind=kLoop, calls=%fused_computation.3 | loop fusion | flops 196608 | bytes 1179649 | tf_op jit(solution)/shard_map/jit(_where)/select_n | solution.py:374
  (35 shorter events, 0.2 us)
Async XLA Ops:
  2.7 13.4 %copy-start.2 = (bf16[1,64,3072]{2,1,0:T(8,128)(2,1)S(1)}, bf16[1,64,3072]{2,1,0:T(8,128)(2,1)}, u32[]{:S(2)}) copy-start(bf16[1,64,3072]{2,1,0:T(8,128)(2,1)} %param.7) | copy-start | bytes 1179652
  2.7 52.6 %all-to-all-start = ((bf16[8,2,64,384]{3,2,1,0:T(8,128)(2,1)}), bf16[8,2,64,384]{3,2,1,0:T(8,128)(2,1)S(1)}, u32[]{:S(2)}, u32[]{:S(2)}) async-start(bf16[8,2,64,384]{3,2,1,0:T(8,128)(2,1)} %shard_map.86), calls=%async_computation | async-start | bytes 1572864 | tf_op jit(solution)/shard_map/all_to_all | solution.py:302
  16.2 2.5 %collective-permute-start = (bf16[80,3072]{1,0:T(8,128)(2,1)S(1)}, bf16[80,3072]{1,0:T(8,128)(2,1)S(1)}, u32[]{:S(2)}, u32[]{:S(2)}) collective-permute-start(bf16[80,3072]{1,0:T(8,128)(2,1)S(1)} %pad_maximum_fusion), channel_id=1, source_target_pairs={{248,168},{249,217},{250,42},{251,11},{252,140},{253,125},{254,46}... | collective-permute-start | bytes 1474568 | tf_op jit(solution)/shard_map/ppermute | solution.py:301
  18.7 36.7 %copy-start.5 = (bf16[80,3072]{1,0:T(8,128)(2,1)}, bf16[80,3072]{1,0:T(8,128)(2,1)S(1)}, u32[]{:S(2)}) copy-start(bf16[80,3072]{1,0:T(8,128)(2,1)S(1)} %collective-permute-done) | copy-start | bytes 1474564
  55.4 11.0 %collective-permute-start.2 = (bf16[4,2,64,384]{3,2,1,0:T(8,128)(2,1)S(1)}, bf16[4,2,64,384]{3,2,1,0:T(8,128)(2,1)}, u32[]{:S(2)}, u32[]{:S(2)}) collective-permute-start(bf16[4,2,64,384]{3,2,1,0:T(8,128)(2,1)S(1)} %get-tuple-element.24), channel_id=1, source_target_pairs={{240,192},{241,49},{242,50},{243,243},{244,244},{245,53},{246,54},... | collective-permute-start | bytes 1179656 | tf_op jit(solution)/shard_map/ppermute | solution.py:301
  56.7 9.7 %collective-permute-start.1 = (bf16[4,2,64,384]{3,2,1,0:T(8,128)(2,1)S(1)}, bf16[4,2,64,384]{3,2,1,0:T(8,128)(2,1)S(1)}, u32[]{:S(2)}, u32[]{:S(2)}) collective-permute-start(bf16[4,2,64,384]{3,2,1,0:T(8,128)(2,1)S(1)} %get-tuple-element.25), channel_id=1, source_target_pairs={{240,224},{241,177},{242,178},{243,243},{244,244},{245,181},{246,1... | collective-permute-start | bytes 1179656 | tf_op jit(solution)/shard_map/ppermute | solution.py:301
  66.4 29.5 %collective-permute-start.4 = (bf16[8,2,64,384]{3,2,1,0:T(8,128)(2,1)S(1)}, bf16[8,2,64,384]{3,2,1,0:T(8,128)(2,1)S(1)}, u32[]{:S(2)}, u32[]{:S(2)}) collective-permute-start(bf16[8,2,64,384]{3,2,1,0:T(8,128)(2,1)S(1)} %all-to-all-done.own), channel_id=1, source_target_pairs={{16,0},{17,1},{18,2},{19,3},{20,4},{21,5},{22,6},{23,7},{24,8},{25... | collective-permute-start | bytes 2359304 | tf_op jit(solution)/shard_map/ppermute | solution.py:301
  68.3 27.6 %collective-permute-start.3 = (bf16[8,2,64,384]{3,2,1,0:T(8,128)(2,1)S(1)}, bf16[8,2,64,384]{3,2,1,0:T(8,128)(2,1)S(1)}, u32[]{:S(2)}, u32[]{:S(2)}) collective-permute-start(bf16[8,2,64,384]{3,2,1,0:T(8,128)(2,1)S(1)} %all-to-all-done.own), channel_id=1, source_target_pairs={{0,16},{1,17},{2,18},{3,19},{4,20},{5,21},{6,22},{7,23},{8,24},{9,... | collective-permute-start | bytes 2359304 | tf_op jit(solution)/shard_map/ppermute | solution.py:301
  72.3 19.5 %collective-permute-start.5 = (bf16[4,2,64,384]{3,2,1,0:T(8,128)(2,1)S(1)}, bf16[4,2,64,384]{3,2,1,0:T(8,128)(2,1)}, u32[]{:S(2)}, u32[]{:S(2)}) collective-permute-start(bf16[4,2,64,384]{3,2,1,0:T(8,128)(2,1)S(1)} %collective-permute-done.1), channel_id=1, source_target_pairs={{224,263},{177,262},{178,261},{243,260},{244,259},{181,258},{182,2... | collective-permute-start | bytes 1179656 | tf_op jit(solution)/shard_map/ppermute | solution.py:301
  73.7 21.2 %collective-permute-start.6 = (bf16[4,2,64,384]{3,2,1,0:T(8,128)(2,1)}, bf16[4,2,64,384]{3,2,1,0:T(8,128)(2,1)}, u32[]{:S(2)}, u32[]{:S(2)}) collective-permute-start(bf16[4,2,64,384]{3,2,1,0:T(8,128)(2,1)} %collective-permute-done.2), channel_id=1, source_target_pairs={{192,263},{49,262},{50,261},{243,260},{244,259},{53,258},{54,257},... | collective-permute-start | bytes 1179656 | tf_op jit(solution)/shard_map/ppermute | solution.py:301
  81.8 24.1 %all-to-all-start.1 = ((bf16[8,1,64,384]{3,2,1,0:T(8,128)(2,1)}), bf16[8,1,64,384]{3,2,1,0:T(8,128)(2,1)S(1)}, u32[]{:S(2)}, u32[]{:S(2)}) async-start(bf16[8,1,64,384]{3,2,1,0:T(8,128)(2,1)} %shard_map.87), calls=%async_computation.1 | async-start | bytes 786432 | tf_op jit(solution)/shard_map/all_to_all | solution.py:302
  89.8 11.8 %collective-permute-start.7 = (bf16[8,2,64,384]{3,2,1,0:T(8,128)(2,1)S(1)}, bf16[8,2,64,384]{3,2,1,0:T(8,128)(2,1)}, u32[]{:S(2)}, u32[]{:S(2)}) collective-permute-start(bf16[8,2,64,384]{3,2,1,0:T(8,128)(2,1)S(1)} %all-to-all-done.own), channel_id=1, source_target_pairs={{0,8},{1,9},{2,10},{3,11},{4,12},{5,13},{6,14},{7,15},{8,0},{9,1},... | collective-permute-start | bytes 2359304 | tf_op jit(solution)/shard_map/ppermute | solution.py:301
  97.0 8.8 %collective-permute-start.8 = (bf16[8,2,64,384]{3,2,1,0:T(8,128)(2,1)}, bf16[8,2,64,384]{3,2,1,0:T(8,128)(2,1)}, u32[]{:S(2)}, u32[]{:S(2)}) collective-permute-start(bf16[8,2,64,384]{3,2,1,0:T(8,128)(2,1)} %select_select_fusion), channel_id=1, source_target_pairs={{0,8},{1,9},{2,10},{3,11},{4,12},{5,13},{6,14},{7,15},{8,0},{9,1},... | collective-permute-start | bytes 2359304 | tf_op jit(solution)/shard_map/ppermute | solution.py:301
  99.0 0.7 copy-start.4
  120.4 8.7 %copy-start.6 = (bf16[80,3072]{1,0:T(8,128)(2,1)S(1)}, bf16[80,3072]{1,0:T(8,128)(2,1)}, u32[]{:S(2)}) copy-start(bf16[80,3072]{1,0:T(8,128)(2,1)} %copy-done.5) | copy-start | bytes 1474564
  120.4 9.3 %collective-permute-start.13 = (bf16[2,64,384]{2,1,0:T(8,128)(2,1)S(1)}, bf16[2,64,384]{2,1,0:T(8,128)(2,1)S(1)}, u32[]{:S(2)}, u32[]{:S(2)}) collective-permute-start(bf16[2,64,384]{2,1,0:T(8,128)(2,1)S(1)} %get-tuple-element.26), channel_id=1, source_target_pairs={{248,262},{249,263},{250,256},{251,257},{252,258},{253,259},{254,2... | collective-permute-start | bytes 294920 | tf_op jit(solution)/shard_map/ppermute | solution.py:301
  121.2 8.6 %collective-permute-start.12 = (bf16[2,64,384]{2,1,0:T(8,128)(2,1)S(1)}, bf16[2,64,384]{2,1,0:T(8,128)(2,1)S(1)}, u32[]{:S(2)}, u32[]{:S(2)}) collective-permute-start(bf16[2,64,384]{2,1,0:T(8,128)(2,1)S(1)} %get-tuple-element.27), channel_id=1, source_target_pairs={{248,260},{249,261},{250,262},{251,263},{252,256},{253,257},{254,2... | collective-permute-start | bytes 294920 | tf_op jit(solution)/shard_map/ppermute | solution.py:301
  121.9 7.9 %collective-permute-start.11 = (bf16[2,64,384]{2,1,0:T(8,128)(2,1)S(1)}, bf16[2,64,384]{2,1,0:T(8,128)(2,1)S(1)}, u32[]{:S(2)}, u32[]{:S(2)}) collective-permute-start(bf16[2,64,384]{2,1,0:T(8,128)(2,1)S(1)} %get-tuple-element.28), channel_id=1, source_target_pairs={{248,258},{249,259},{250,260},{251,261},{252,262},{253,263},{254,2... | collective-permute-start | bytes 294920 | tf_op jit(solution)/shard_map/ppermute | solution.py:301
  122.6 7.3 %collective-permute-start.10 = (bf16[2,64,384]{2,1,0:T(8,128)(2,1)S(1)}, bf16[2,64,384]{2,1,0:T(8,128)(2,1)S(1)}, u32[]{:S(2)}, u32[]{:S(2)}) collective-permute-start(bf16[2,64,384]{2,1,0:T(8,128)(2,1)S(1)} %get-tuple-element.29), channel_id=1, source_target_pairs={{248,256},{249,257},{250,258},{251,259},{252,260},{253,261},{254,2... | collective-permute-start | bytes 294920 | tf_op jit(solution)/shard_map/ppermute | solution.py:301
  123.3 27.6 %all-to-all-start.2 = ((bf16[8,64,384]{2,1,0:T(8,128)(2,1)}), bf16[8,64,384]{2,1,0:T(8,128)(2,1)S(1)}, u32[]{:S(2)}, u32[]{:S(2)}) async-start(bf16[8,64,384]{2,1,0:T(8,128)(2,1)} %shard_map.88), calls=%async_computation.2 | async-start | bytes 786432 | tf_op jit(solution)/shard_map/all_to_all | solution.py:302
  129.0 27.9 %collective-permute-start.9 = (bf16[80,3072]{1,0:T(8,128)(2,1)S(1)}, bf16[80,3072]{1,0:T(8,128)(2,1)S(1)}, u32[]{:S(2)}, u32[]{:S(2)}) collective-permute-start(bf16[80,3072]{1,0:T(8,128)(2,1)S(1)} %copy-done.6), channel_id=1, source_target_pairs={{168,256},{217,257},{42,258},{11,259},{140,260},{125,261},{46,262}... | collective-permute-start | bytes 1474568 | tf_op jit(solution)/shard_map/ppermute | solution.py:301
  129.8 0.6 copy-start.7
  129.8 0.7 copy-start.8
  129.8 0.7 copy-start.9
  129.8 0.7 copy-start.10
  132.3 23.9 %collective-permute-start.14 = (bf16[4,64,384]{2,1,0:T(8,128)(2,1)}, bf16[4,64,384]{2,1,0:T(8,128)(2,1)S(1)}, u32[]{:S(2)}, u32[]{:S(2)}) collective-permute-start(bf16[4,64,384]{2,1,0:T(8,128)(2,1)} %get-tuple-element.23), channel_id=1, source_target_pairs={{256,257},{257,256},{258,259},{259,258},{260,261},{261,260},{262,2... | collective-permute-start | bytes 589832 | tf_op jit(solution)/shard_map/ppermute | solution.py:301
  133.5 22.6 %copy-start.3 = (bf16[4,64,384]{2,1,0:T(8,128)(2,1)S(1)}, bf16[4,64,384]{2,1,0:T(8,128)(2,1)}, u32[]{:S(2)}) copy-start(bf16[4,64,384]{2,1,0:T(8,128)(2,1)} %get-tuple-element.22) | copy-start | bytes 589828
  150.8 0.7 copy-start.1
  153.6 11.4 %collective-permute-start.15 = (bf16[1,64,3072]{2,1,0:T(8,128)(2,1)}, bf16[1,64,3072]{2,1,0:T(8,128)(2,1)S(1)}, u32[]{:S(2)}, u32[]{:S(2)}) collective-permute-start(bf16[1,64,3072]{2,1,0:T(8,128)(2,1)} %bitcast.31), channel_id=1, source_target_pairs={{0,8},{1,9},{2,10},{3,11},{4,12},{5,13},{6,14},{7,15},{8,16},{9,17... | collective-permute-start | bytes 1179656 | tf_op jit(solution)/shard_map/ppermute | solution.py:301
  157.0 0.8 copy-start

commit v4 on v3

--- a/solution.py
+++ b/solution.py
@@ -16,9 +16,10 @@
 AXES = ("frame", "head")
 EXITS_A = ((2, 3), (3, 2), (3, 2), (3, 3))
 EXITS_B = ((0, 3), (3, 0), (3, 0), (3, 3))
-EXITS_STEP = ((2, 2), (1, 3), (2, 0), (0, 0), (0, 2), (3, 1), (2, 0), (1, 3))
+EXITS_STEP = ((2, 2), (1, 3), (2, 0), (0, 0), (0, 2), (3, 1), (0, 0), (0, 2))
 MARK_LENT = 2 * 10**9
 MARK_PIECES = 16 * 10**9
+MARK_TRADED = 8 * 10**9
 
 
 def head_split_kernel(groups, width, flip_ref, *refs):
@@ -224,35 +225,52 @@
     )(value)
 
 
-def blend_lent_kernel(groups, rows, width, order_ref, before_ref, returned_ref, fresh_ref, out_ref):
-    first = order_ref[groups] == 1
-    high = before_ref[rows : rows + 1, :width].astype(jnp.float32)
-    low = before_ref[rows + 1 : rows + 2, :width].astype(jnp.float32)
-    level = (high * 32.0 + low) / LEVELS
-    keep_share = 1.0 - 0.5 * level
-    push_share = 0.5 + level
-    for group in range(groups):
-        block = order_ref[group]
-        columns = slice(group * width, (group + 1) * width)
-        entry = (
-            keep_share * before_ref[:rows, columns].astype(jnp.float32)
-            + push_share * returned_ref[block].astype(jnp.float32)
-        ).astype(jnp.bfloat16)
-        out_ref[:, columns] = jnp.where(first, fresh_ref[:, columns], entry)
-
-
-def blend_lent(order, before, returned, fresh):
-    groups, rows, width = returned.shape
-    shape = (rows, groups * width)
-    return pl.pallas_call(
-        functools.partial(blend_lent_kernel, groups, rows, width),
-        out_shape=jax.ShapeDtypeStruct(shape, jnp.bfloat16),
-        in_specs=[pl.BlockSpec(memory_space=pltpu.SMEM)] + [pl.BlockSpec(memory_space=pltpu.VMEM)] * 3,
-        out_specs=pl.BlockSpec(memory_space=pltpu.VMEM),
-        cost_estimate=pl.CostEstimate(
-            flops=3 * rows * groups * width, bytes_accessed=6 * rows * groups * width, transcendentals=0
-        ),
-    )(order, before, returned, fresh)
+def enter_kernel(groups, rows, width, order_ref, before, kept, got, fresh, advanced, out, lat, mixed, entry, sem):
+    def fetch(*moves):
+        copies = [pltpu.make_async_copy(*move, sem.at[index]) for index, move in enumerate(moves)]
+        for copy in copies:
+            copy.start()
+        for copy in copies:
+            copy.wait()
+
+    @pl.when(order_ref[groups] == 1)
+    def _():
+        fetch((fresh, out))
+
+    @pl.when(order_ref[groups] == 2)
+    def _():
+        part = groups // 2
+        fetch((before, lat), (kept, mixed.at[pl.ds(0, part)]), (got, mixed.at[pl.ds(part, part)]))
+        level = (lat[rows : rows + 1, :width].astype(jnp.float32) * 32.0 + lat[rows + 1 : rows + 2, :width].astype(jnp.float32)) / LEVELS
+        keep_share = 1.0 - 0.5 * level
+        push_share = 0.5 + level
+        for group in range(groups):
+            columns = slice(group * width, (group + 1) * width)
+            entry[:, columns] = (
+                keep_share * lat[:rows, columns].astype(jnp.float32)
+                + push_share * mixed[order_ref[group]].astype(jnp.float32)
+            ).astype(jnp.bfloat16)
+        fetch((entry, out))
+
+
+def enter(order, before, kept, got, fresh, advanced):
+    part, rows, width = kept.shape
+    groups = 2 * part
+    return pl.pallas_call(
+        functools.partial(enter_kernel, groups, rows, width),
+        out_shape=jax.ShapeDtypeStruct(advanced.shape, advanced.dtype),
+        in_specs=[pl.BlockSpec(memory_space=pltpu.SMEM)] + [pl.BlockSpec(memory_space=pl.ANY)] * 5,
+        out_specs=pl.BlockSpec(memory_space=pl.ANY),
+        input_output_aliases={5: 0},
+        scratch_shapes=[
+            pltpu.VMEM(before.shape, jnp.bfloat16),
+            pltpu.VMEM((groups, rows, width), jnp.bfloat16),
+            pltpu.VMEM((rows, groups * width), jnp.bfloat16),
+            pltpu.SemaphoreType.DMA((3,)),
+        ],
+        compiler_params=pltpu.CompilerParams(vmem_limit_bytes=40 * 1024 * 1024),
+        cost_estimate=pl.CostEstimate(flops=0, bytes_accessed=0, transcendentals=0),
+    )(order, before, kept, got, fresh, advanced)
 
 
 def with_step(latents, timesteps):
@@ -360,18 +378,19 @@
         )
         for shift in range(mid)
     ]
-    before = mark(send(before, [(lent_to[a], half * heads + a) for a in range(heads)]), MARK_LENT)
+    before = send(before, [(lent_to[a], half * heads + a) for a in range(heads)])
     parity = z % 2
     kept, given = sort_pieces(parity[None], pieces, MARK_PIECES)
-    got = send(given, [(half * heads + a, half * heads + (a ^ 1)) for a in range(heads)])
+    given, before = lax.optimization_barrier((given, before))
+    got = mark(send(given, [(half * heads + a, half * heads + (a ^ 1)) for a in range(heads)]), MARK_TRADED)
     denoised = blend(flip, shares, latents[0], returned)[None]
     groups = jnp.arange(heads)
     source = jnp.where(groups % 2 == parity, z, z + 1 - 2 * parity)
     order = ((source - groups) % heads) // 2 + jnp.where(groups % 2 == parity, 0, mid)
-    order = jnp.concatenate([order, (frame == 0).astype(order.dtype)[None]])
-    entering = blend_lent(order, before, jnp.concatenate([kept, got]), fresh)[None]
+    entering = jnp.where(frame == 0, 1, jnp.where(frame == half, 2, 0))
+    order = jnp.concatenate([order, entering[None]]).astype(jnp.int32)
     advanced = send(denoised, straight([(f, f + 1) for f in range(frames - 1) if f != half - 1]))
-    return (denoised, jnp.where((frame == 0) | (frame == half), entering, advanced))
+    return (denoised, enter(order, before, kept, got, fresh, advanced[0])[None])
 
 
 def solution(mesh):

time: 168 us -> 167 us (level)
  waiting for transfers between devices: 74.2 us -> 78.5 us
  other arithmetic: 5.6 us -> 2.45 us
    ppermute x16, waiting for transfers between devices: 16.2 us -> 20.6 us  [per_device(): send = lambda value, moves: lax.ppermute(value, AXES, moves)]
    select_n x1 -> x0, other arithmetic: 1.78 us -> none  [per_device(): jnp.where((frame == 0) | (frame == half), entering, advanced)]
    unnamed x23 -> x24, local copies, waits for them, and re-layouts: 3.9 us -> 3.87 us
  transfers between devices with their start and end apart: 19 -> 19, of which waited for: 6 -> 6; matrix products, arithmetic and copies ran while one was open for 4% -> 3% of each run, Pallas kernels for 5% -> 3%
where the time goes in v4:
time: 167 us; the launch traced here: 166 us
  waiting for transfers between devices  78.5 us (47%)
  starting transfers between devices  54.5 us (33%)
  Pallas kernels  21.8 us (13%)
  local copies, waits for them, and re-layouts  6.75 us (4%)
  between operations  2.48 us (1%)
  other arithmetic  2.45 us (1%)
    all_to_all x3, waiting for transfers between devices, per_device(): lax.all_to_all(value, 'head', split_axis=0, concat_axis=0, tiled=True)  57.9 us
    ppermute x16, starting transfers between devices, per_device(): send = lambda value, moves: lax.ppermute(value, AXES, moves)  28 us
    all_to_all x3, starting transfers between devices, per_device(): lax.all_to_all(value, 'head', split_axis=0, concat_axis=0, tiled=True)  26.5 us
    ppermute x16, waiting for transfers between devices, per_device(): send = lambda value, moves: lax.ppermute(value, AXES, moves)  20.6 us
    pallas_call x1, Pallas kernels, attend(): pl.pallas_call(functools.partial(attention_kernel, blocks, pairs, rows),...  13.5 us
    unnamed x24, local copies, waits for them, and re-layouts  3.87 us
    pallas_call x2, Pallas kernels, head_split(): pl.pallas_call(functools.partial(head_split_kernel, groups, width), out_s...  3.85 us
  transfers between devices with their start and end apart: 19, of which 6 were waited for; matrix products, arithmetic and copies ran while one was open for 3% of the time, Pallas kernels for 3%

profile of v4, /device:TPU:24, one launch (start us, length us, event | category | flops | bytes accessed | tf_op | source)
XLA Modules:
  0.0 166.5 jit_solution(1176807202088344399)
XLA Ops:
  0.6 2.1 %shard_map.86 = bf16[8,2,64,384]{3,2,1,0:T(8,128)(2,1)} custom-call(s32[1]{0:T(128)} %bitcast.flip_ref, bf16[64,3072]{1,0:T(8,128)(2,1)} %bitcast.30, bf16[64,3072]{1,0:T(8,128)(2,1)} %bitcast.31), custom_call_target="tpu_custom_call" | custom-call | bytes 1572864 | tf_op jit(solution)/shard_map/pallas_call | solution.py:39
  2.7 12.7 %all-to-all-start = ((bf16[8,2,64,384]{3,2,1,0:T(8,128)(2,1)}), bf16[8,2,64,384]{3,2,1,0:T(8,128)(2,1)S(1)}, u32[]{:S(2)}, u32[]{:S(2)}) async-start(bf16[8,2,64,384]{3,2,1,0:T(8,128)(2,1)} %shard_map.86), calls=%async_computation | async-start | bytes 1572864 | tf_op jit(solution)/shard_map/all_to_all | solution.py:320
  16.1 0.1 select_convert_fusion
  16.2 0.7 collective-permute-start
  16.9 1.8 %shard_map.87 = bf16[8,1,64,384]{3,2,1,0:T(8,128)(2,1)} custom-call(s32[1]{0:T(128)} %bitcast.flip_ref, bf16[64,3072]{1,0:T(8,128)(2,1)} %bitcast.32), custom_call_target="tpu_custom_call" | custom-call | bytes 786432 | tf_op jit(solution)/shard_map/pallas_call | solution.py:39
  18.7 36.6 %all-to-all-done.own = bf16[8,2,64,384]{3,2,1,0:T(8,128)(2,1)S(1)} async-done(((bf16[8,2,64,384]{3,2,1,0:T(8,128)(2,1)}), bf16[8,2,64,384]{3,2,1,0:T(8,128)(2,1)S(1)}, u32[]{:S(2)}, u32[]{:S(2)}) %all-to-all-start) | async-done | bytes 786464 | tf_op jit(solution)/shard_map/all_to_all | solution.py:320
  55.3 0.1 fusion.4
  55.4 1.3 collective-permute-start.2
  56.7 0.7 collective-permute-start.1
  57.4 9.0 %collective-permute-done.2 = bf16[4,2,64,384]{3,2,1,0:T(8,128)(2,1)} collective-permute-done((bf16[4,2,64,384]{3,2,1,0:T(8,128)(2,1)S(1)}, bf16[4,2,64,384]{3,2,1,0:T(8,128)(2,1)}, u32[]{:S(2)}, u32[]{:S(2)}) %collective-permute-start.2) | collective-permute-done | bytes 393248 | tf_op jit(solution)/shard_map/ppermute | solution.py:319
  66.4 1.9 %collective-permute-start.4 = (bf16[8,2,64,384]{3,2,1,0:T(8,128)(2,1)S(1)}, bf16[8,2,64,384]{3,2,1,0:T(8,128)(2,1)S(1)}, u32[]{:S(2)}, u32[]{:S(2)}) collective-permute-start(bf16[8,2,64,384]{3,2,1,0:T(8,128)(2,1)S(1)} %all-to-all-done.own), channel_id=1, source_target_pairs={{16,0},{17,1},{18,2},{19,3},{20,4},{21,5},{22,6},{23,7},{24,8},{25... | collective-permute-start | bytes 2359304 | tf_op jit(solution)/shard_map/ppermute | solution.py:319
  68.3 3.9 %collective-permute-start.3 = (bf16[8,2,64,384]{3,2,1,0:T(8,128)(2,1)S(1)}, bf16[8,2,64,384]{3,2,1,0:T(8,128)(2,1)S(1)}, u32[]{:S(2)}, u32[]{:S(2)}) collective-permute-start(bf16[8,2,64,384]{3,2,1,0:T(8,128)(2,1)S(1)} %all-to-all-done.own), channel_id=1, source_target_pairs={{0,16},{1,17},{2,18},{3,19},{4,20},{5,21},{6,22},{7,23},{8,24},{9,... | collective-permute-start | bytes 2359304 | tf_op jit(solution)/shard_map/ppermute | solution.py:319
  72.3 1.4 collective-permute-start.5
  73.7 8.1 %collective-permute-start.6 = (bf16[4,2,64,384]{3,2,1,0:T(8,128)(2,1)}, bf16[4,2,64,384]{3,2,1,0:T(8,128)(2,1)}, u32[]{:S(2)}, u32[]{:S(2)}) collective-permute-start(bf16[4,2,64,384]{3,2,1,0:T(8,128)(2,1)} %collective-permute-done.2), channel_id=1, source_target_pairs={{192,263},{49,262},{50,261},{243,260},{244,259},{53,258},{54,257},... | collective-permute-start | bytes 1179656 | tf_op jit(solution)/shard_map/ppermute | solution.py:319
  81.8 8.1 %all-to-all-start.1 = ((bf16[8,1,64,384]{3,2,1,0:T(8,128)(2,1)}), bf16[8,1,64,384]{3,2,1,0:T(8,128)(2,1)S(1)}, u32[]{:S(2)}, u32[]{:S(2)}) async-start(bf16[8,1,64,384]{3,2,1,0:T(8,128)(2,1)} %shard_map.87), calls=%async_computation.1 | async-start | bytes 786432 | tf_op jit(solution)/shard_map/all_to_all | solution.py:320
  89.8 1.9 %collective-permute-start.7 = (bf16[8,2,64,384]{3,2,1,0:T(8,128)(2,1)S(1)}, bf16[8,2,64,384]{3,2,1,0:T(8,128)(2,1)}, u32[]{:S(2)}, u32[]{:S(2)}) collective-permute-start(bf16[8,2,64,384]{3,2,1,0:T(8,128)(2,1)S(1)} %all-to-all-done.own), channel_id=1, source_target_pairs={{0,8},{1,9},{2,10},{3,11},{4,12},{5,13},{6,14},{7,15},{8,0},{9,1},... | collective-permute-start | bytes 2359304 | tf_op jit(solution)/shard_map/ppermute | solution.py:319
  91.8 1.0 constant_dynamic-update-slice_fusion.1
  92.8 2.1 %collective-permute-done.6 = bf16[4,2,64,384]{3,2,1,0:T(8,128)(2,1)} collective-permute-done((bf16[4,2,64,384]{3,2,1,0:T(8,128)(2,1)}, bf16[4,2,64,384]{3,2,1,0:T(8,128)(2,1)}, u32[]{:S(2)}, u32[]{:S(2)}) %collective-permute-start.6) | collective-permute-done | bytes 393248 | tf_op jit(solution)/shard_map/ppermute | solution.py:319
  94.9 1.1 constant_dynamic-update-slice_fusion.cross
  96.0 1.0 select_select_fusion
  97.0 1.9 %collective-permute-start.8 = (bf16[8,2,64,384]{3,2,1,0:T(8,128)(2,1)}, bf16[8,2,64,384]{3,2,1,0:T(8,128)(2,1)}, u32[]{:S(2)}, u32[]{:S(2)}) collective-permute-start(bf16[8,2,64,384]{3,2,1,0:T(8,128)(2,1)} %select_select_fusion), channel_id=1, source_target_pairs={{0,8},{1,9},{2,10},{3,11},{4,12},{5,13},{6,14},{7,15},{8,0},{9,1},... | collective-permute-start | bytes 2359304 | tf_op jit(solution)/shard_map/ppermute | solution.py:319
  99.1 0.6 copy-done.4
  99.7 0.6 fusion.5
  101.0 0.6 and_select_fusion.5.picks_ref
  101.7 4.1 %all-to-all-done.1.q_ref = bf16[8,1,64,384]{3,2,1,0:T(8,128)(2,1)S(1)} async-done(((bf16[8,1,64,384]{3,2,1,0:T(8,128)(2,1)}), bf16[8,1,64,384]{3,2,1,0:T(8,128)(2,1)S(1)}, u32[]{:S(2)}, u32[]{:S(2)}) %all-to-all-start.1) | async-done | bytes 393248 | tf_op jit(solution)/shard_map/all_to_all | solution.py:320
  105.8 13.5 %shard_map.88 = bf16[8,64,384]{2,1,0:T(8,128)(2,1)} custom-call(s32[5]{0:T(128)S(1)} %and_select_fusion.5.picks_ref, bf16[8,1,64,384]{3,2,1,0:T(8,128)(2,1)S(1)} %all-to-all-done.1.q_ref, bf16[8,2,64,384]{3,2,1,0:T(8,128)(2,1)S(1)} %all-to-all-done.own, bf16[8,2,64,384]{3,2,1,0:T(8,128)(2,1)S(1)} %collective-permute-done.3.back2, ...), custom_call_target="tpu_custom_call" | custom-call | flops 2013265920 | bytes 4718592 | tf_op jit(solution)/shard_map/pallas_call | solution.py:168
  119.4 1.1 dynamic-slice_bitcast_fusion
  120.5 0.8 collective-permute-start.12
  121.3 0.7 collective-permute-start.11
  122.0 0.7 collective-permute-start.10
  122.6 0.7 collective-permute-start.9
  123.3 5.8 %all-to-all-start.2 = ((bf16[8,64,384]{2,1,0:T(8,128)(2,1)}), bf16[8,64,384]{2,1,0:T(8,128)(2,1)S(1)}, u32[]{:S(2)}, u32[]{:S(2)}) async-start(bf16[8,64,384]{2,1,0:T(8,128)(2,1)} %shard_map.88), calls=%async_computation.2 | async-start | bytes 786432 | tf_op jit(solution)/shard_map/all_to_all | solution.py:320
  129.1 0.7 collective-permute-start.13
  129.9 0.6 copy-done.7
  130.5 0.0 copy-done.8
  130.5 0.0 copy-done.9
  130.5 0.0 copy-done.10
  130.5 1.8 %shard_map.90 = (bf16[4,64,384]{2,1,0:T(8,128)(2,1)}, bf16[4,64,384]{2,1,0:T(8,128)(2,1)}) custom-call(s32[1]{0:T(128)} %bitcast.10.parity_ref, bf16[2,64,384]{2,1,0:T(8,128)(2,1)} %copy-done.10, bf16[2,64,384]{2,1,0:T(8,128)(2,1)} %copy-done.9, bf16[2,64,384]{2,1,0:T(8,128)(2,1)} %copy-done.8, bf16[2,64,384]{2,1,0:T(8,128)(2,1)} %copy-done.7), custom_call_target="tpu_custom_call" | custom-call | flops 16000000000 | tf_op jit(solution)/shard_map/pallas_call | solution.py:292
  132.4 0.7 collective-permute-start.14
  133.0 0.6 pad_maximum_fusion.1.share_ref
  133.6 0.1 pad_add_fusion.order_ref
  133.7 17.2 %all-to-all-done.2.returned_ref = bf16[8,64,384]{2,1,0:T(8,128)(2,1)S(1)} async-done(((bf16[8,64,384]{2,1,0:T(8,128)(2,1)}), bf16[8,64,384]{2,1,0:T(8,128)(2,1)S(1)}, u32[]{:S(2)}, u32[]{:S(2)}) %all-to-all-start.2) | async-done | bytes 393248 | tf_op jit(solution)/shard_map/all_to_all | solution.py:320
  150.8 0.7 copy-done.2
  151.6 2.0 %shard_map.89 = bf16[64,3072]{1,0:T(8,128)(2,1)} custom-call(s32[1]{0:T(128)} %bitcast.flip_ref, f32[2]{0:T(128)} %pad_maximum_fusion.1.share_ref, bf16[64,3072]{1,0:T(8,128)(2,1)} %bitcast.28, bf16[8,64,384]{2,1,0:T(8,128)(2,1)} %copy-done.2), custom_call_target="tpu_custom_call" | custom-call | flops 589824 | bytes 1179648 | tf_op jit(solution)/shard_map/pallas_call | solution.py:203
  153.6 2.0 %collective-permute-start.15 = (bf16[1,64,3072]{2,1,0:T(8,128)(2,1)}, bf16[1,64,3072]{2,1,0:T(8,128)(2,1)S(1)}, u32[]{:S(2)}, u32[]{:S(2)}) collective-permute-start(bf16[1,64,3072]{2,1,0:T(8,128)(2,1)} %bitcast.33), channel_id=1, source_target_pairs={{0,8},{1,9},{2,10},{3,11},{4,12},{5,13},{6,14},{7,15},{8,16},{9,17... | collective-permute-start | bytes 1179656 | tf_op jit(solution)/shard_map/ppermute | solution.py:319
  155.7 9.5 %collective-permute-done.15 = bf16[1,64,3072]{2,1,0:T(8,128)(2,1)S(1)} collective-permute-done((bf16[1,64,3072]{2,1,0:T(8,128)(2,1)}, bf16[1,64,3072]{2,1,0:T(8,128)(2,1)S(1)}, u32[]{:S(2)}, u32[]{:S(2)}) %collective-permute-start.15) | collective-permute-done | bytes 393248 | tf_op jit(solution)/shard_map/ppermute | solution.py:319
  165.2 0.6 shard_map.92
  165.7 0.7 copy.16
  (34 shorter events, 0.1 us)
Async XLA Ops:
  2.7 13.4 %copy-start.3 = (bf16[1,64,3072]{2,1,0:T(8,128)(2,1)S(1)}, bf16[1,64,3072]{2,1,0:T(8,128)(2,1)}, u32[]{:S(2)}) copy-start(bf16[1,64,3072]{2,1,0:T(8,128)(2,1)} %param.7) | copy-start | bytes 1179652
  2.7 52.6 %all-to-all-start = ((bf16[8,2,64,384]{3,2,1,0:T(8,128)(2,1)}), bf16[8,2,64,384]{3,2,1,0:T(8,128)(2,1)S(1)}, u32[]{:S(2)}, u32[]{:S(2)}) async-start(bf16[8,2,64,384]{3,2,1,0:T(8,128)(2,1)} %shard_map.86), calls=%async_computation | async-start | bytes 1572864 | tf_op jit(solution)/shard_map/all_to_all | solution.py:320
  16.2 2.5 %collective-permute-start = (bf16[80,3072]{1,0:T(8,128)(2,1)S(1)}, bf16[80,3072]{1,0:T(8,128)(2,1)S(1)}, u32[]{:S(2)}, u32[]{:S(2)}) collective-permute-start(bf16[80,3072]{1,0:T(8,128)(2,1)S(1)} %pad_maximum_fusion), channel_id=1, source_target_pairs={{248,168},{249,217},{250,42},{251,11},{252,140},{253,125},{254,14}... | collective-permute-start | bytes 1474568 | tf_op jit(solution)/shard_map/ppermute | solution.py:319
  18.7 36.7 %copy-start.5 = (bf16[80,3072]{1,0:T(8,128)(2,1)}, bf16[80,3072]{1,0:T(8,128)(2,1)S(1)}, u32[]{:S(2)}) copy-start(bf16[80,3072]{1,0:T(8,128)(2,1)S(1)} %collective-permute-done) | copy-start | bytes 1474564
  55.4 11.0 %collective-permute-start.2 = (bf16[4,2,64,384]{3,2,1,0:T(8,128)(2,1)S(1)}, bf16[4,2,64,384]{3,2,1,0:T(8,128)(2,1)}, u32[]{:S(2)}, u32[]{:S(2)}) collective-permute-start(bf16[4,2,64,384]{3,2,1,0:T(8,128)(2,1)S(1)} %get-tuple-element.28), channel_id=1, source_target_pairs={{240,192},{241,49},{242,50},{243,243},{244,244},{245,53},{246,54},... | collective-permute-start | bytes 1179656 | tf_op jit(solution)/shard_map/ppermute | solution.py:319
  56.7 9.7 %collective-permute-start.1 = (bf16[4,2,64,384]{3,2,1,0:T(8,128)(2,1)S(1)}, bf16[4,2,64,384]{3,2,1,0:T(8,128)(2,1)S(1)}, u32[]{:S(2)}, u32[]{:S(2)}) collective-permute-start(bf16[4,2,64,384]{3,2,1,0:T(8,128)(2,1)S(1)} %get-tuple-element.29), channel_id=1, source_target_pairs={{240,224},{241,177},{242,178},{243,243},{244,244},{245,181},{246,1... | collective-permute-start | bytes 1179656 | tf_op jit(solution)/shard_map/ppermute | solution.py:319
  66.4 29.5 %collective-permute-start.4 = (bf16[8,2,64,384]{3,2,1,0:T(8,128)(2,1)S(1)}, bf16[8,2,64,384]{3,2,1,0:T(8,128)(2,1)S(1)}, u32[]{:S(2)}, u32[]{:S(2)}) collective-permute-start(bf16[8,2,64,384]{3,2,1,0:T(8,128)(2,1)S(1)} %all-to-all-done.own), channel_id=1, source_target_pairs={{16,0},{17,1},{18,2},{19,3},{20,4},{21,5},{22,6},{23,7},{24,8},{25... | collective-permute-start | bytes 2359304 | tf_op jit(solution)/shard_map/ppermute | solution.py:319
  68.3 27.6 %collective-permute-start.3 = (bf16[8,2,64,384]{3,2,1,0:T(8,128)(2,1)S(1)}, bf16[8,2,64,384]{3,2,1,0:T(8,128)(2,1)S(1)}, u32[]{:S(2)}, u32[]{:S(2)}) collective-permute-start(bf16[8,2,64,384]{3,2,1,0:T(8,128)(2,1)S(1)} %all-to-all-done.own), channel_id=1, source_target_pairs={{0,16},{1,17},{2,18},{3,19},{4,20},{5,21},{6,22},{7,23},{8,24},{9,... | collective-permute-start | bytes 2359304 | tf_op jit(solution)/shard_map/ppermute | solution.py:319
  72.3 19.5 %collective-permute-start.5 = (bf16[4,2,64,384]{3,2,1,0:T(8,128)(2,1)S(1)}, bf16[4,2,64,384]{3,2,1,0:T(8,128)(2,1)}, u32[]{:S(2)}, u32[]{:S(2)}) collective-permute-start(bf16[4,2,64,384]{3,2,1,0:T(8,128)(2,1)S(1)} %collective-permute-done.1), channel_id=1, source_target_pairs={{224,263},{177,262},{178,261},{243,260},{244,259},{181,258},{182,2... | collective-permute-start | bytes 1179656 | tf_op jit(solution)/shard_map/ppermute | solution.py:319
  73.7 21.2 %collective-permute-start.6 = (bf16[4,2,64,384]{3,2,1,0:T(8,128)(2,1)}, bf16[4,2,64,384]{3,2,1,0:T(8,128)(2,1)}, u32[]{:S(2)}, u32[]{:S(2)}) collective-permute-start(bf16[4,2,64,384]{3,2,1,0:T(8,128)(2,1)} %collective-permute-done.2), channel_id=1, source_target_pairs={{192,263},{49,262},{50,261},{243,260},{244,259},{53,258},{54,257},... | collective-permute-start | bytes 1179656 | tf_op jit(solution)/shard_map/ppermute | solution.py:319
  81.8 24.1 %all-to-all-start.1 = ((bf16[8,1,64,384]{3,2,1,0:T(8,128)(2,1)}), bf16[8,1,64,384]{3,2,1,0:T(8,128)(2,1)S(1)}, u32[]{:S(2)}, u32[]{:S(2)}) async-start(bf16[8,1,64,384]{3,2,1,0:T(8,128)(2,1)} %shard_map.87), calls=%async_computation.1 | async-start | bytes 786432 | tf_op jit(solution)/shard_map/all_to_all | solution.py:320
  89.8 11.9 %collective-permute-start.7 = (bf16[8,2,64,384]{3,2,1,0:T(8,128)(2,1)S(1)}, bf16[8,2,64,384]{3,2,1,0:T(8,128)(2,1)}, u32[]{:S(2)}, u32[]{:S(2)}) collective-permute-start(bf16[8,2,64,384]{3,2,1,0:T(8,128)(2,1)S(1)} %all-to-all-done.own), channel_id=1, source_target_pairs={{0,8},{1,9},{2,10},{3,11},{4,12},{5,13},{6,14},{7,15},{8,0},{9,1},... | collective-permute-start | bytes 2359304 | tf_op jit(solution)/shard_map/ppermute | solution.py:319
  97.0 8.8 %collective-permute-start.8 = (bf16[8,2,64,384]{3,2,1,0:T(8,128)(2,1)}, bf16[8,2,64,384]{3,2,1,0:T(8,128)(2,1)}, u32[]{:S(2)}, u32[]{:S(2)}) collective-permute-start(bf16[8,2,64,384]{3,2,1,0:T(8,128)(2,1)} %select_select_fusion), channel_id=1, source_target_pairs={{0,8},{1,9},{2,10},{3,11},{4,12},{5,13},{6,14},{7,15},{8,0},{9,1},... | collective-permute-start | bytes 2359304 | tf_op jit(solution)/shard_map/ppermute | solution.py:319
  99.0 0.7 copy-start.4
  120.5 8.6 %copy-start.6 = (bf16[80,3072]{1,0:T(8,128)(2,1)S(1)}, bf16[80,3072]{1,0:T(8,128)(2,1)}, u32[]{:S(2)}) copy-start(bf16[80,3072]{1,0:T(8,128)(2,1)} %copy-done.5) | copy-start | bytes 1474564
  120.5 9.3 %collective-permute-start.12 = (bf16[2,64,384]{2,1,0:T(8,128)(2,1)S(1)}, bf16[2,64,384]{2,1,0:T(8,128)(2,1)S(1)}, u32[]{:S(2)}, u32[]{:S(2)}) collective-permute-start(bf16[2,64,384]{2,1,0:T(8,128)(2,1)S(1)} %get-tuple-element.30), channel_id=1, source_target_pairs={{248,262},{249,263},{250,256},{251,257},{252,258},{253,259},{254,2... | collective-permute-start | bytes 294920 | tf_op jit(solution)/shard_map/ppermute | solution.py:319
  121.3 8.5 %collective-permute-start.11 = (bf16[2,64,384]{2,1,0:T(8,128)(2,1)S(1)}, bf16[2,64,384]{2,1,0:T(8,128)(2,1)S(1)}, u32[]{:S(2)}, u32[]{:S(2)}) collective-permute-start(bf16[2,64,384]{2,1,0:T(8,128)(2,1)S(1)} %get-tuple-element.31), channel_id=1, source_target_pairs={{248,260},{249,261},{250,262},{251,263},{252,256},{253,257},{254,2... | collective-permute-start | bytes 294920 | tf_op jit(solution)/shard_map/ppermute | solution.py:319
  122.0 7.9 %collective-permute-start.10 = (bf16[2,64,384]{2,1,0:T(8,128)(2,1)S(1)}, bf16[2,64,384]{2,1,0:T(8,128)(2,1)S(1)}, u32[]{:S(2)}, u32[]{:S(2)}) collective-permute-start(bf16[2,64,384]{2,1,0:T(8,128)(2,1)S(1)} %get-tuple-element.32), channel_id=1, source_target_pairs={{248,258},{249,259},{250,260},{251,261},{252,262},{253,263},{254,2... | collective-permute-start | bytes 294920 | tf_op jit(solution)/shard_map/ppermute | solution.py:319
  122.6 7.2 %collective-permute-start.9 = (bf16[2,64,384]{2,1,0:T(8,128)(2,1)S(1)}, bf16[2,64,384]{2,1,0:T(8,128)(2,1)S(1)}, u32[]{:S(2)}, u32[]{:S(2)}) collective-permute-start(bf16[2,64,384]{2,1,0:T(8,128)(2,1)S(1)} %get-tuple-element.33), channel_id=1, source_target_pairs={{248,256},{249,257},{250,258},{251,259},{252,260},{253,261},{254,2... | collective-permute-start | bytes 294920 | tf_op jit(solution)/shard_map/ppermute | solution.py:319
  123.3 27.5 %all-to-all-start.2 = ((bf16[8,64,384]{2,1,0:T(8,128)(2,1)}), bf16[8,64,384]{2,1,0:T(8,128)(2,1)S(1)}, u32[]{:S(2)}, u32[]{:S(2)}) async-start(bf16[8,64,384]{2,1,0:T(8,128)(2,1)} %shard_map.88), calls=%async_computation.2 | async-start | bytes 786432 | tf_op jit(solution)/shard_map/all_to_all | solution.py:320
  129.1 3.3 %collective-permute-start.13 = (bf16[80,3072]{1,0:T(8,128)(2,1)S(1)}, bf16[80,3072]{1,0:T(8,128)(2,1)S(1)}, u32[]{:S(2)}, u32[]{:S(2)}) collective-permute-start(bf16[80,3072]{1,0:T(8,128)(2,1)S(1)} %copy-done.6), channel_id=1, source_target_pairs={{168,256},{217,257},{42,258},{11,259},{140,260},{125,261},{14,262}... | collective-permute-start | bytes 1474568 | tf_op jit(solution)/shard_map/ppermute | solution.py:319
  129.8 0.6 copy-start.7
  129.8 0.7 copy-start.8
  129.9 0.7 copy-start.9
  129.9 0.7 copy-start.10
  132.4 23.3 %collective-permute-start.14 = (bf16[4,64,384]{2,1,0:T(8,128)(2,1)}, bf16[4,64,384]{2,1,0:T(8,128)(2,1)S(1)}, u32[]{:S(2)}, u32[]{:S(2)}) collective-permute-start(bf16[4,64,384]{2,1,0:T(8,128)(2,1)} %get-tuple-element.27), channel_id=1, source_target_pairs={{256,257},{257,256},{258,259},{259,258},{260,261},{261,260},{262,2... | collective-permute-start | bytes 589832 | tf_op jit(solution)/shard_map/ppermute | solution.py:319
  150.8 0.7 copy-start.2
  153.6 11.5 %copy-start = (bf16[64,3072]{1,0:T(8,128)(2,1)S(1)}, bf16[64,3072]{1,0:T(8,128)(2,1)}, u32[]{:S(2)}) copy-start(bf16[64,3072]{1,0:T(8,128)(2,1)} %fresh.1) | copy-start | bytes 1179652
  153.6 11.5 %copy-start.1 = (bf16[4,64,384]{2,1,0:T(8,128)(2,1)S(1)}, bf16[4,64,384]{2,1,0:T(8,128)(2,1)}, u32[]{:S(2)}) copy-start(bf16[4,64,384]{2,1,0:T(8,128)(2,1)} %get-tuple-element.26.kept) | copy-start | bytes 589828
  153.6 11.5 %collective-permute-start.15 = (bf16[1,64,3072]{2,1,0:T(8,128)(2,1)}, bf16[1,64,3072]{2,1,0:T(8,128)(2,1)S(1)}, u32[]{:S(2)}, u32[]{:S(2)}) collective-permute-start(bf16[1,64,3072]{2,1,0:T(8,128)(2,1)} %bitcast.33), channel_id=1, source_target_pairs={{0,8},{1,9},{2,10},{3,11},{4,12},{5,13},{6,14},{7,15},{8,16},{9,17... | collective-permute-start | bytes 1179656 | tf_op jit(solution)/shard_map/ppermute | solution.py:319

commit v5 on v4

--- a/solution.py
+++ b/solution.py
@@ -59,11 +59,10 @@
         columns = pl.ds(pair * PAIR, PAIR)
         return [
             pltpu.make_async_copy(
-                source.at[block, which, :, columns],
-                buf.at[pair, slot, pl.ds(block * per_block, per_block), pl.ds(0, PAIR)],
+                source.at[:, which, :, columns],
+                buf.at[pair, slot, :, :, pl.ds(0, PAIR)],
                 sem.at[pair, slot, which],
             )
-            for block in range(blocks)
         ]
 
     def fetch(source, slot, pair):
@@ -82,7 +81,7 @@
             def _(pair=pair, slot=slot):
                 for copy in copies(own, slot, pair, 0, k_buf):
                     copy.start()
-                v_buf[pair, slot] = jnp.zeros((span, 2 * PAIR), jnp.bfloat16)
+                v_buf[pair, slot] = jnp.zeros((blocks, per_block, 2 * PAIR), jnp.bfloat16)
 
             @pl.when(picks_ref[slot] == 1)
             def _(pair=pair, slot=slot):
@@ -96,7 +95,7 @@
         for slot in range(SLOTS):
             @pl.when(picks_ref[slot] > 0)
             def _(pair=pair, slot=slot):
-                v_buf[pair, slot, :, PAIR:] = jnp.ones((span, PAIR), jnp.bfloat16)
+                v_buf[pair, slot, :, :, PAIR:] = jnp.ones((blocks, per_block, PAIR), jnp.bfloat16)
 
     def arrive(pair):
         for slot in range(SLOTS):
@@ -122,7 +121,7 @@
         high = None
         for slot in range(SLOTS):
             found = lax.dot_general(
-                both, k_buf[step // chunks, slot], (((1,), (1,)), ((), ())), preferred_element_type=jnp.float32
+                both, k_buf[step // chunks, slot].reshape(span, PAIR), (((1,), (1,)), ((), ())), preferred_element_type=jnp.float32
             )
             score[slot] = found
             for start in range(0, span, 128):
@@ -134,7 +133,7 @@
         total = None
         for slot in range(SLOTS):
             weights = jnp.exp2((score[slot] - high) * (HD ** -0.5 * LOG2E)).astype(jnp.bfloat16)
-            part = jnp.dot(weights, v_buf[step // chunks, slot], preferred_element_type=jnp.float32)
+            part = jnp.dot(weights, v_buf[step // chunks, slot].reshape(span, 2 * PAIR), preferred_element_type=jnp.float32)
             total = part if total is None else total + part
         mixed = total[:, :PAIR] / total[:, PAIR:]
         mixed = jnp.where(lane < HD, mixed[:rows], mixed[rows:]).astype(jnp.bfloat16)
@@ -172,8 +171,8 @@
         + [pl.BlockSpec(memory_space=pl.ANY)] * 6,
         out_specs=pl.BlockSpec(memory_space=pltpu.VMEM),
         scratch_shapes=[
-            pltpu.VMEM((pairs, SLOTS, span, PAIR), jnp.bfloat16),
-            pltpu.VMEM((pairs, SLOTS, span, 2 * PAIR), jnp.bfloat16),
+            pltpu.VMEM((pairs, SLOTS, blocks, per_block, PAIR), jnp.bfloat16),
+            pltpu.VMEM((pairs, SLOTS, blocks, per_block, 2 * PAIR), jnp.bfloat16),
             pltpu.VMEM((SLOTS, 2 * rows, span), jnp.float32),
             pltpu.VMEM((SLOTS, 2 * rows, span), jnp.float32),
             pltpu.SemaphoreType.DMA((pairs, SLOTS, 2)),
@@ -300,6 +299,7 @@
 
 def per_device(frames, heads, latents, queries, keys, values, fresh, timesteps, window):
     frame = lax.axis_index("frame")
+    core = frame % 2
     half = frames // 2
     flip = (frame >= half).astype(jnp.int32)[None]
 
@@ -324,7 +324,14 @@
     lent_to = [(y * 8 + x * 2 + 1) * heads + a for a, (x, y) in enumerate(EXITS_STEP)]
     lending = [((half - 1) * heads + a, lent_to[a]) for a in range(heads)]
     before = send(with_step(latents[0], timesteps), lending)
-    own, query, before = lax.optimization_barrier((own, query, before))
+    offsets = jnp.arange(-REACH, REACH + 1)
+    target = frame + offsets
+    allowed = (
+        (target >= 0) & (target < frames) & (offsets >= -window[0, 0]) & (offsets <= window[0, 1])
+    )
+    other = jnp.where(offsets % 2 == 0, (target < half) != (frame < half), target // 2 != frame // 2)
+    picks = jnp.where(allowed, jnp.where(other, 2, 1), 0).astype(jnp.int32)
+    own, query, before, picks = lax.optimization_barrier((own, query, before, picks))
 
     mid = heads // 2
     edge = (half - 2, half - 1, half, half + 1)
@@ -344,7 +351,6 @@
 
     near_a, on_a = through(own[:mid], EXITS_A)
     near_b, on_b = through(own[mid:], EXITS_B)
-    core = frame % 2
     pairwise = straight([(f, f ^ 1) for f in range(frames)])
     chip = send(own, pairwise)
     own, near_a, near_b = lax.optimization_barrier((own, near_a, near_b))
@@ -357,13 +363,6 @@
     near_a, near_b, query = lax.optimization_barrier((near_a, near_b, query))
     query = exchange(query)
 
-    offsets = jnp.arange(-REACH, REACH + 1)
-    target = frame + offsets
-    allowed = (
-        (target >= 0) & (target < frames) & (offsets >= -window[0, 0]) & (offsets <= window[0, 1])
-    )
-    other = jnp.where(offsets % 2 == 0, (target < half) != (frame < half), target // 2 != frame // 2)
-    picks = jnp.where(allowed, jnp.where(other, 2, 1), 0).astype(jnp.int32)
     attended = attend(picks, query, own, back2, next2, cross, chip, far)
     z = lax.axis_index("head")
     levels = timesteps.astype(jnp.float32) / LEVELS

time: 167 us -> 167 us (level)
  no operation moved by 1% of the time
where the time goes in v5:
time: 167 us; the launch traced here: 166 us
  waiting for transfers between devices  78.2 us (47%)
  starting transfers between devices  54.5 us (33%)
  Pallas kernels  21.7 us (13%)
  local copies, waits for them, and re-layouts  6.75 us (4%)
  between operations  2.47 us (1%)
  other arithmetic  2.45 us (1%)
    all_to_all x3, waiting for transfers between devices, per_device(): lax.all_to_all(value, 'head', split_axis=0, concat_axis=0, tiled=True)  57.6 us
    ppermute x16, starting transfers between devices, per_device(): send = lambda value, moves: lax.ppermute(value, AXES, moves)  28 us
    all_to_all x3, starting transfers between devices, per_device(): lax.all_to_all(value, 'head', split_axis=0, concat_axis=0, tiled=True)  26.5 us
    ppermute x16, waiting for transfers between devices, per_device(): send = lambda value, moves: lax.ppermute(value, AXES, moves)  20.6 us
    pallas_call x1, Pallas kernels, attend(): pl.pallas_call(functools.partial(attention_kernel, blocks, pairs, rows),...  13.5 us
    unnamed x24, local copies, waits for them, and re-layouts  3.87 us
    pallas_call x2, Pallas kernels, head_split(): pl.pallas_call(functools.partial(head_split_kernel, groups, width), out_s...  3.85 us
  transfers between devices with their start and end apart: 19, of which 6 were waited for; matrix products, arithmetic and copies ran while one was open for 3% of the time, Pallas kernels for 3%

profile of v5, /device:TPU:24, one launch (start us, length us, event | category | flops | bytes accessed | tf_op | source)
XLA Modules:
  0.0 166.1 jit_solution(2765465933663303033)
XLA Ops:
  0.6 2.1 %shard_map.86 = bf16[8,2,64,384]{3,2,1,0:T(8,128)(2,1)} custom-call(s32[1]{0:T(128)} %bitcast.flip_ref, bf16[64,3072]{1,0:T(8,128)(2,1)} %bitcast.30, bf16[64,3072]{1,0:T(8,128)(2,1)} %bitcast.31), custom_call_target="tpu_custom_call" | custom-call | bytes 1572864 | tf_op jit(solution)/shard_map/pallas_call | solution.py:39
  2.7 12.7 %all-to-all-start = ((bf16[8,2,64,384]{3,2,1,0:T(8,128)(2,1)}), bf16[8,2,64,384]{3,2,1,0:T(8,128)(2,1)S(1)}, u32[]{:S(2)}, u32[]{:S(2)}) async-start(bf16[8,2,64,384]{3,2,1,0:T(8,128)(2,1)} %shard_map.86), calls=%async_computation | async-start | bytes 1572864 | tf_op jit(solution)/shard_map/all_to_all | solution.py:320
  16.1 0.1 select_convert_fusion
  16.2 0.7 collective-permute-start
  16.9 0.6 copy-done.4
  17.6 0.6 fusion.5
  18.9 1.8 %shard_map.87 = bf16[8,1,64,384]{3,2,1,0:T(8,128)(2,1)} custom-call(s32[1]{0:T(128)} %bitcast.flip_ref, bf16[64,3072]{1,0:T(8,128)(2,1)} %bitcast.32), custom_call_target="tpu_custom_call" | custom-call | bytes 786432 | tf_op jit(solution)/shard_map/pallas_call | solution.py:39
  20.7 0.6 and_select_fusion.5.picks_ref
  21.3 34.0 %all-to-all-done.own = bf16[8,2,64,384]{3,2,1,0:T(8,128)(2,1)S(1)} async-done(((bf16[8,2,64,384]{3,2,1,0:T(8,128)(2,1)}), bf16[8,2,64,384]{3,2,1,0:T(8,128)(2,1)S(1)}, u32[]{:S(2)}, u32[]{:S(2)}) %all-to-all-start) | async-done | bytes 786464 | tf_op jit(solution)/shard_map/all_to_all | solution.py:320
  55.3 0.1 fusion.4
  55.4 1.3 collective-permute-start.2
  56.7 0.7 collective-permute-start.1
  57.4 9.0 %collective-permute-done.2 = bf16[4,2,64,384]{3,2,1,0:T(8,128)(2,1)} collective-permute-done((bf16[4,2,64,384]{3,2,1,0:T(8,128)(2,1)S(1)}, bf16[4,2,64,384]{3,2,1,0:T(8,128)(2,1)}, u32[]{:S(2)}, u32[]{:S(2)}) %collective-permute-start.2) | collective-permute-done | bytes 393248 | tf_op jit(solution)/shard_map/ppermute | solution.py:319
  66.4 1.9 %collective-permute-start.4 = (bf16[8,2,64,384]{3,2,1,0:T(8,128)(2,1)S(1)}, bf16[8,2,64,384]{3,2,1,0:T(8,128)(2,1)S(1)}, u32[]{:S(2)}, u32[]{:S(2)}) collective-permute-start(bf16[8,2,64,384]{3,2,1,0:T(8,128)(2,1)S(1)} %all-to-all-done.own), channel_id=1, source_target_pairs={{16,0},{17,1},{18,2},{19,3},{20,4},{21,5},{22,6},{23,7},{24,8},{25... | collective-permute-start | bytes 2359304 | tf_op jit(solution)/shard_map/ppermute | solution.py:319
  68.3 3.9 %collective-permute-start.3 = (bf16[8,2,64,384]{3,2,1,0:T(8,128)(2,1)S(1)}, bf16[8,2,64,384]{3,2,1,0:T(8,128)(2,1)S(1)}, u32[]{:S(2)}, u32[]{:S(2)}) collective-permute-start(bf16[8,2,64,384]{3,2,1,0:T(8,128)(2,1)S(1)} %all-to-all-done.own), channel_id=1, source_target_pairs={{0,16},{1,17},{2,18},{3,19},{4,20},{5,21},{6,22},{7,23},{8,24},{9,... | collective-permute-start | bytes 2359304 | tf_op jit(solution)/shard_map/ppermute | solution.py:319
  72.3 1.4 collective-permute-start.5
  73.7 8.1 %collective-permute-start.6 = (bf16[4,2,64,384]{3,2,1,0:T(8,128)(2,1)}, bf16[4,2,64,384]{3,2,1,0:T(8,128)(2,1)}, u32[]{:S(2)}, u32[]{:S(2)}) collective-permute-start(bf16[4,2,64,384]{3,2,1,0:T(8,128)(2,1)} %collective-permute-done.2), channel_id=1, source_target_pairs={{192,263},{49,262},{50,261},{243,260},{244,259},{53,258},{54,257},... | collective-permute-start | bytes 1179656 | tf_op jit(solution)/shard_map/ppermute | solution.py:319
  81.8 8.1 %all-to-all-start.1 = ((bf16[8,1,64,384]{3,2,1,0:T(8,128)(2,1)}), bf16[8,1,64,384]{3,2,1,0:T(8,128)(2,1)S(1)}, u32[]{:S(2)}, u32[]{:S(2)}) async-start(bf16[8,1,64,384]{3,2,1,0:T(8,128)(2,1)} %shard_map.87), calls=%async_computation.1 | async-start | bytes 786432 | tf_op jit(solution)/shard_map/all_to_all | solution.py:320
  89.8 1.9 %collective-permute-start.7 = (bf16[8,2,64,384]{3,2,1,0:T(8,128)(2,1)S(1)}, bf16[8,2,64,384]{3,2,1,0:T(8,128)(2,1)}, u32[]{:S(2)}, u32[]{:S(2)}) collective-permute-start(bf16[8,2,64,384]{3,2,1,0:T(8,128)(2,1)S(1)} %all-to-all-done.own), channel_id=1, source_target_pairs={{0,8},{1,9},{2,10},{3,11},{4,12},{5,13},{6,14},{7,15},{8,0},{9,1},... | collective-permute-start | bytes 2359304 | tf_op jit(solution)/shard_map/ppermute | solution.py:319
  91.8 1.0 constant_dynamic-update-slice_fusion.1
  92.8 2.1 %collective-permute-done.6 = bf16[4,2,64,384]{3,2,1,0:T(8,128)(2,1)} collective-permute-done((bf16[4,2,64,384]{3,2,1,0:T(8,128)(2,1)}, bf16[4,2,64,384]{3,2,1,0:T(8,128)(2,1)}, u32[]{:S(2)}, u32[]{:S(2)}) %collective-permute-start.6) | collective-permute-done | bytes 393248 | tf_op jit(solution)/shard_map/ppermute | solution.py:319
  94.9 1.1 constant_dynamic-update-slice_fusion.cross
  96.0 1.0 select_select_fusion
  97.0 1.9 %collective-permute-start.8 = (bf16[8,2,64,384]{3,2,1,0:T(8,128)(2,1)}, bf16[8,2,64,384]{3,2,1,0:T(8,128)(2,1)}, u32[]{:S(2)}, u32[]{:S(2)}) collective-permute-start(bf16[8,2,64,384]{3,2,1,0:T(8,128)(2,1)} %select_select_fusion), channel_id=1, source_target_pairs={{0,8},{1,9},{2,10},{3,11},{4,12},{5,13},{6,14},{7,15},{8,0},{9,1},... | collective-permute-start | bytes 2359304 | tf_op jit(solution)/shard_map/ppermute | solution.py:319
  99.0 6.8 %all-to-all-done.1.q_ref = bf16[8,1,64,384]{3,2,1,0:T(8,128)(2,1)S(1)} async-done(((bf16[8,1,64,384]{3,2,1,0:T(8,128)(2,1)}), bf16[8,1,64,384]{3,2,1,0:T(8,128)(2,1)S(1)}, u32[]{:S(2)}, u32[]{:S(2)}) %all-to-all-start.1) | async-done | bytes 393248 | tf_op jit(solution)/shard_map/all_to_all | solution.py:320
  105.8 13.5 %shard_map.88 = bf16[8,64,384]{2,1,0:T(8,128)(2,1)} custom-call(s32[5]{0:T(128)S(1)} %and_select_fusion.5.picks_ref, bf16[8,1,64,384]{3,2,1,0:T(8,128)(2,1)S(1)} %all-to-all-done.1.q_ref, bf16[8,2,64,384]{3,2,1,0:T(8,128)(2,1)S(1)} %all-to-all-done.own, bf16[8,2,64,384]{3,2,1,0:T(8,128)(2,1)S(1)} %collective-permute-done.3.back2, ...), custom_call_target="tpu_custom_call" | custom-call | flops 2013265920 | bytes 4718592 | tf_op jit(solution)/shard_map/pallas_call | solution.py:167
  119.3 1.1 dynamic-slice_bitcast_fusion
  120.4 0.8 collective-permute-start.12
  121.2 0.7 collective-permute-start.11
  121.9 0.7 collective-permute-start.10
  122.6 0.7 collective-permute-start.9
  123.3 5.8 %all-to-all-start.2 = ((bf16[8,64,384]{2,1,0:T(8,128)(2,1)}), bf16[8,64,384]{2,1,0:T(8,128)(2,1)S(1)}, u32[]{:S(2)}, u32[]{:S(2)}) async-start(bf16[8,64,384]{2,1,0:T(8,128)(2,1)} %shard_map.88), calls=%async_computation.2 | async-start | bytes 786432 | tf_op jit(solution)/shard_map/all_to_all | solution.py:320
  129.1 0.7 collective-permute-start.13
  129.9 0.6 copy-done.7
  130.4 0.0 copy-done.8
  130.5 0.0 copy-done.9
  130.5 0.0 copy-done.10
  130.5 1.8 %shard_map.90 = (bf16[4,64,384]{2,1,0:T(8,128)(2,1)}, bf16[4,64,384]{2,1,0:T(8,128)(2,1)}) custom-call(s32[1]{0:T(128)} %bitcast.10.parity_ref, bf16[2,64,384]{2,1,0:T(8,128)(2,1)} %copy-done.10, bf16[2,64,384]{2,1,0:T(8,128)(2,1)} %copy-done.9, bf16[2,64,384]{2,1,0:T(8,128)(2,1)} %copy-done.8, bf16[2,64,384]{2,1,0:T(8,128)(2,1)} %copy-done.7), custom_call_target="tpu_custom_call" | custom-call | flops 16000000000 | tf_op jit(solution)/shard_map/pallas_call | solution.py:291
  132.3 0.7 collective-permute-start.14
  133.0 0.6 pad_maximum_fusion.1.share_ref
  133.6 0.1 pad_add_fusion.order_ref
  133.6 16.8 %all-to-all-done.2.returned_ref = bf16[8,64,384]{2,1,0:T(8,128)(2,1)S(1)} async-done(((bf16[8,64,384]{2,1,0:T(8,128)(2,1)}), bf16[8,64,384]{2,1,0:T(8,128)(2,1)S(1)}, u32[]{:S(2)}, u32[]{:S(2)}) %all-to-all-start.2) | async-done | bytes 393248 | tf_op jit(solution)/shard_map/all_to_all | solution.py:320
  150.5 0.7 copy-done.2
  151.2 2.0 %shard_map.89 = bf16[64,3072]{1,0:T(8,128)(2,1)} custom-call(s32[1]{0:T(128)} %bitcast.flip_ref, f32[2]{0:T(128)} %pad_maximum_fusion.1.share_ref, bf16[64,3072]{1,0:T(8,128)(2,1)} %bitcast.28, bf16[8,64,384]{2,1,0:T(8,128)(2,1)} %copy-done.2), custom_call_target="tpu_custom_call" | custom-call | flops 589824 | bytes 1179648 | tf_op jit(solution)/shard_map/pallas_call | solution.py:202
  153.2 2.0 %collective-permute-start.15 = (bf16[1,64,3072]{2,1,0:T(8,128)(2,1)}, bf16[1,64,3072]{2,1,0:T(8,128)(2,1)S(1)}, u32[]{:S(2)}, u32[]{:S(2)}) collective-permute-start(bf16[1,64,3072]{2,1,0:T(8,128)(2,1)} %bitcast.33), channel_id=1, source_target_pairs={{0,8},{1,9},{2,10},{3,11},{4,12},{5,13},{6,14},{7,15},{8,16},{9,17... | collective-permute-start | bytes 1179656 | tf_op jit(solution)/shard_map/ppermute | solution.py:319
  155.3 9.5 %collective-permute-done.15 = bf16[1,64,3072]{2,1,0:T(8,128)(2,1)S(1)} collective-permute-done((bf16[1,64,3072]{2,1,0:T(8,128)(2,1)}, bf16[1,64,3072]{2,1,0:T(8,128)(2,1)S(1)}, u32[]{:S(2)}, u32[]{:S(2)}) %collective-permute-start.15) | collective-permute-done | bytes 393248 | tf_op jit(solution)/shard_map/ppermute | solution.py:319
  164.8 0.6 shard_map.92
  165.4 0.7 copy.16
  (34 shorter events, 0.1 us)
Async XLA Ops:
  2.7 13.4 %copy-start.3 = (bf16[1,64,3072]{2,1,0:T(8,128)(2,1)S(1)}, bf16[1,64,3072]{2,1,0:T(8,128)(2,1)}, u32[]{:S(2)}) copy-start(bf16[1,64,3072]{2,1,0:T(8,128)(2,1)} %param.7) | copy-start | bytes 1179652
  2.7 52.6 %all-to-all-start = ((bf16[8,2,64,384]{3,2,1,0:T(8,128)(2,1)}), bf16[8,2,64,384]{3,2,1,0:T(8,128)(2,1)S(1)}, u32[]{:S(2)}, u32[]{:S(2)}) async-start(bf16[8,2,64,384]{3,2,1,0:T(8,128)(2,1)} %shard_map.86), calls=%async_computation | async-start | bytes 1572864 | tf_op jit(solution)/shard_map/all_to_all | solution.py:320
  16.2 5.1 %collective-permute-start = (bf16[80,3072]{1,0:T(8,128)(2,1)S(1)}, bf16[80,3072]{1,0:T(8,128)(2,1)S(1)}, u32[]{:S(2)}, u32[]{:S(2)}) collective-permute-start(bf16[80,3072]{1,0:T(8,128)(2,1)S(1)} %pad_maximum_fusion), channel_id=1, source_target_pairs={{248,168},{249,217},{250,42},{251,11},{252,140},{253,125},{254,14}... | collective-permute-start | bytes 1474568 | tf_op jit(solution)/shard_map/ppermute | solution.py:319
  16.9 0.7 copy-start.4
  21.3 34.1 %copy-start.5 = (bf16[80,3072]{1,0:T(8,128)(2,1)}, bf16[80,3072]{1,0:T(8,128)(2,1)S(1)}, u32[]{:S(2)}) copy-start(bf16[80,3072]{1,0:T(8,128)(2,1)S(1)} %collective-permute-done) | copy-start | bytes 1474564
  55.4 11.0 %collective-permute-start.2 = (bf16[4,2,64,384]{3,2,1,0:T(8,128)(2,1)S(1)}, bf16[4,2,64,384]{3,2,1,0:T(8,128)(2,1)}, u32[]{:S(2)}, u32[]{:S(2)}) collective-permute-start(bf16[4,2,64,384]{3,2,1,0:T(8,128)(2,1)S(1)} %get-tuple-element.30), channel_id=1, source_target_pairs={{240,192},{241,49},{242,50},{243,243},{244,244},{245,53},{246,54},... | collective-permute-start | bytes 1179656 | tf_op jit(solution)/shard_map/ppermute | solution.py:319
  56.7 9.7 %collective-permute-start.1 = (bf16[4,2,64,384]{3,2,1,0:T(8,128)(2,1)S(1)}, bf16[4,2,64,384]{3,2,1,0:T(8,128)(2,1)S(1)}, u32[]{:S(2)}, u32[]{:S(2)}) collective-permute-start(bf16[4,2,64,384]{3,2,1,0:T(8,128)(2,1)S(1)} %get-tuple-element.31), channel_id=1, source_target_pairs={{240,224},{241,177},{242,178},{243,243},{244,244},{245,181},{246,1... | collective-permute-start | bytes 1179656 | tf_op jit(solution)/shard_map/ppermute | solution.py:319
  66.4 29.5 %collective-permute-start.4 = (bf16[8,2,64,384]{3,2,1,0:T(8,128)(2,1)S(1)}, bf16[8,2,64,384]{3,2,1,0:T(8,128)(2,1)S(1)}, u32[]{:S(2)}, u32[]{:S(2)}) collective-permute-start(bf16[8,2,64,384]{3,2,1,0:T(8,128)(2,1)S(1)} %all-to-all-done.own), channel_id=1, source_target_pairs={{16,0},{17,1},{18,2},{19,3},{20,4},{21,5},{22,6},{23,7},{24,8},{25... | collective-permute-start | bytes 2359304 | tf_op jit(solution)/shard_map/ppermute | solution.py:319
  68.3 27.6 %collective-permute-start.3 = (bf16[8,2,64,384]{3,2,1,0:T(8,128)(2,1)S(1)}, bf16[8,2,64,384]{3,2,1,0:T(8,128)(2,1)S(1)}, u32[]{:S(2)}, u32[]{:S(2)}) collective-permute-start(bf16[8,2,64,384]{3,2,1,0:T(8,128)(2,1)S(1)} %all-to-all-done.own), channel_id=1, source_target_pairs={{0,16},{1,17},{2,18},{3,19},{4,20},{5,21},{6,22},{7,23},{8,24},{9,... | collective-permute-start | bytes 2359304 | tf_op jit(solution)/shard_map/ppermute | solution.py:319
  72.3 19.5 %collective-permute-start.5 = (bf16[4,2,64,384]{3,2,1,0:T(8,128)(2,1)S(1)}, bf16[4,2,64,384]{3,2,1,0:T(8,128)(2,1)}, u32[]{:S(2)}, u32[]{:S(2)}) collective-permute-start(bf16[4,2,64,384]{3,2,1,0:T(8,128)(2,1)S(1)} %collective-permute-done.1), channel_id=1, source_target_pairs={{224,263},{177,262},{178,261},{243,260},{244,259},{181,258},{182,2... | collective-permute-start | bytes 1179656 | tf_op jit(solution)/shard_map/ppermute | solution.py:319
  73.7 21.2 %collective-permute-start.6 = (bf16[4,2,64,384]{3,2,1,0:T(8,128)(2,1)}, bf16[4,2,64,384]{3,2,1,0:T(8,128)(2,1)}, u32[]{:S(2)}, u32[]{:S(2)}) collective-permute-start(bf16[4,2,64,384]{3,2,1,0:T(8,128)(2,1)} %collective-permute-done.2), channel_id=1, source_target_pairs={{192,263},{49,262},{50,261},{243,260},{244,259},{53,258},{54,257},... | collective-permute-start | bytes 1179656 | tf_op jit(solution)/shard_map/ppermute | solution.py:319
  81.8 24.1 %all-to-all-start.1 = ((bf16[8,1,64,384]{3,2,1,0:T(8,128)(2,1)}), bf16[8,1,64,384]{3,2,1,0:T(8,128)(2,1)S(1)}, u32[]{:S(2)}, u32[]{:S(2)}) async-start(bf16[8,1,64,384]{3,2,1,0:T(8,128)(2,1)} %shard_map.87), calls=%async_computation.1 | async-start | bytes 786432 | tf_op jit(solution)/shard_map/all_to_all | solution.py:320
  89.8 9.2 %collective-permute-start.7 = (bf16[8,2,64,384]{3,2,1,0:T(8,128)(2,1)S(1)}, bf16[8,2,64,384]{3,2,1,0:T(8,128)(2,1)}, u32[]{:S(2)}, u32[]{:S(2)}) collective-permute-start(bf16[8,2,64,384]{3,2,1,0:T(8,128)(2,1)S(1)} %all-to-all-done.own), channel_id=1, source_target_pairs={{0,8},{1,9},{2,10},{3,11},{4,12},{5,13},{6,14},{7,15},{8,0},{9,1},... | collective-permute-start | bytes 2359304 | tf_op jit(solution)/shard_map/ppermute | solution.py:319
  97.0 8.8 %collective-permute-start.8 = (bf16[8,2,64,384]{3,2,1,0:T(8,128)(2,1)}, bf16[8,2,64,384]{3,2,1,0:T(8,128)(2,1)}, u32[]{:S(2)}, u32[]{:S(2)}) collective-permute-start(bf16[8,2,64,384]{3,2,1,0:T(8,128)(2,1)} %select_select_fusion), channel_id=1, source_target_pairs={{0,8},{1,9},{2,10},{3,11},{4,12},{5,13},{6,14},{7,15},{8,0},{9,1},... | collective-permute-start | bytes 2359304 | tf_op jit(solution)/shard_map/ppermute | solution.py:319
  120.4 8.6 %copy-start.6 = (bf16[80,3072]{1,0:T(8,128)(2,1)S(1)}, bf16[80,3072]{1,0:T(8,128)(2,1)}, u32[]{:S(2)}) copy-start(bf16[80,3072]{1,0:T(8,128)(2,1)} %copy-done.5) | copy-start | bytes 1474564
  120.4 9.3 %collective-permute-start.12 = (bf16[2,64,384]{2,1,0:T(8,128)(2,1)S(1)}, bf16[2,64,384]{2,1,0:T(8,128)(2,1)S(1)}, u32[]{:S(2)}, u32[]{:S(2)}) collective-permute-start(bf16[2,64,384]{2,1,0:T(8,128)(2,1)S(1)} %get-tuple-element.32), channel_id=1, source_target_pairs={{248,262},{249,263},{250,256},{251,257},{252,258},{253,259},{254,2... | collective-permute-start | bytes 294920 | tf_op jit(solution)/shard_map/ppermute | solution.py:319
  121.2 8.6 %collective-permute-start.11 = (bf16[2,64,384]{2,1,0:T(8,128)(2,1)S(1)}, bf16[2,64,384]{2,1,0:T(8,128)(2,1)S(1)}, u32[]{:S(2)}, u32[]{:S(2)}) collective-permute-start(bf16[2,64,384]{2,1,0:T(8,128)(2,1)S(1)} %get-tuple-element.33), channel_id=1, source_target_pairs={{248,260},{249,261},{250,262},{251,263},{252,256},{253,257},{254,2... | collective-permute-start | bytes 294920 | tf_op jit(solution)/shard_map/ppermute | solution.py:319
  121.9 7.9 %collective-permute-start.10 = (bf16[2,64,384]{2,1,0:T(8,128)(2,1)S(1)}, bf16[2,64,384]{2,1,0:T(8,128)(2,1)S(1)}, u32[]{:S(2)}, u32[]{:S(2)}) collective-permute-start(bf16[2,64,384]{2,1,0:T(8,128)(2,1)S(1)} %get-tuple-element.34), channel_id=1, source_target_pairs={{248,258},{249,259},{250,260},{251,261},{252,262},{253,263},{254,2... | collective-permute-start | bytes 294920 | tf_op jit(solution)/shard_map/ppermute | solution.py:319
  122.6 7.2 %collective-permute-start.9 = (bf16[2,64,384]{2,1,0:T(8,128)(2,1)S(1)}, bf16[2,64,384]{2,1,0:T(8,128)(2,1)S(1)}, u32[]{:S(2)}, u32[]{:S(2)}) collective-permute-start(bf16[2,64,384]{2,1,0:T(8,128)(2,1)S(1)} %get-tuple-element.35), channel_id=1, source_target_pairs={{248,256},{249,257},{250,258},{251,259},{252,260},{253,261},{254,2... | collective-permute-start | bytes 294920 | tf_op jit(solution)/shard_map/ppermute | solution.py:319
  123.3 27.2 %all-to-all-start.2 = ((bf16[8,64,384]{2,1,0:T(8,128)(2,1)}), bf16[8,64,384]{2,1,0:T(8,128)(2,1)S(1)}, u32[]{:S(2)}, u32[]{:S(2)}) async-start(bf16[8,64,384]{2,1,0:T(8,128)(2,1)} %shard_map.88), calls=%async_computation.2 | async-start | bytes 786432 | tf_op jit(solution)/shard_map/all_to_all | solution.py:320
  129.1 3.3 %collective-permute-start.13 = (bf16[80,3072]{1,0:T(8,128)(2,1)S(1)}, bf16[80,3072]{1,0:T(8,128)(2,1)S(1)}, u32[]{:S(2)}, u32[]{:S(2)}) collective-permute-start(bf16[80,3072]{1,0:T(8,128)(2,1)S(1)} %copy-done.6), channel_id=1, source_target_pairs={{168,256},{217,257},{42,258},{11,259},{140,260},{125,261},{14,262}... | collective-permute-start | bytes 1474568 | tf_op jit(solution)/shard_map/ppermute | solution.py:319
  129.8 0.6 copy-start.7
  129.8 0.7 copy-start.8
  129.8 0.7 copy-start.9
  129.8 0.7 copy-start.10
  132.3 22.9 %collective-permute-start.14 = (bf16[4,64,384]{2,1,0:T(8,128)(2,1)}, bf16[4,64,384]{2,1,0:T(8,128)(2,1)S(1)}, u32[]{:S(2)}, u32[]{:S(2)}) collective-permute-start(bf16[4,64,384]{2,1,0:T(8,128)(2,1)} %get-tuple-element.29), channel_id=1, source_target_pairs={{256,257},{257,256},{258,259},{259,258},{260,261},{261,260},{262,2... | collective-permute-start | bytes 589832 | tf_op jit(solution)/shard_map/ppermute | solution.py:319
  150.5 0.7 copy-start.2
  153.2 11.5 %copy-start = (bf16[64,3072]{1,0:T(8,128)(2,1)S(1)}, bf16[64,3072]{1,0:T(8,128)(2,1)}, u32[]{:S(2)}) copy-start(bf16[64,3072]{1,0:T(8,128)(2,1)} %fresh.1) | copy-start | bytes 1179652
  153.2 11.5 %copy-start.1 = (bf16[4,64,384]{2,1,0:T(8,128)(2,1)S(1)}, bf16[4,64,384]{2,1,0:T(8,128)(2,1)}, u32[]{:S(2)}) copy-start(bf16[4,64,384]{2,1,0:T(8,128)(2,1)} %get-tuple-element.28.kept) | copy-start | bytes 589828
  153.2 11.5 %collective-permute-start.15 = (bf16[1,64,3072]{2,1,0:T(8,128)(2,1)}, bf16[1,64,3072]{2,1,0:T(8,128)(2,1)S(1)}, u32[]{:S(2)}, u32[]{:S(2)}) collective-permute-start(bf16[1,64,3072]{2,1,0:T(8,128)(2,1)} %bitcast.33), channel_id=1, source_target_pairs={{0,8},{1,9},{2,10},{3,11},{4,12},{5,13},{6,14},{7,15},{8,16},{9,17... | collective-permute-start | bytes 1179656 | tf_op jit(solution)/shard_map/ppermute | solution.py:319
